TPU v7x, 32 devices: a whole 2x2x4 slice. The times are simulated.
32 devices in a mesh: slab: 8 (over z, x), freq: 4 (over y, core).
Axes of the slice: x: 2, y: 2, z: 4, core: 2. Of those that a mesh axis runs over, the one named last changes fastest.
Arguments:
- source: bfloat16 [4, 2, 3, 64, 64, 128], P('freq', None, None, 'slab'), may hold values from -6 to 6
- omega: float32 [4], P('freq'), may hold values from 0.2 to 5
- sigma_blocks: float32 [256], replicated, may hold values from 0.25 to 4
- block_ids: int32 [64, 64, 128], P('slab'), may hold values from 0 to 255
- rec_owner: int32 [1024, 1], P('slab'), may hold values from 0 to 7; in each aligned block of 128 rows (0 to 127, 128 to 255, ...) at most 32 rows name the same one
- rec_edge: int32 [1024], P('slab'), may hold values from 0 to 196607
- observed: float32 [4, 2, 1024], P('freq', None, 'slab'), may hold values from -4 to 4
Outputs:
- forward_field: float32 [4, 2, 3, 64, 64, 128], P('freq', None, None, 'slab')
- adjoint_field: float32 [4, 2, 3, 64, 64, 128], P('freq', None, None, 'slab')
- gradient: float32 [256], replicated
Inputs may be any that keep to these rules, and one draw needn't show every extreme that they name: `rec_owner`: among the receiver rows of one slab device no slab is named more than 32 times; in some device's rows one slab is named exactly 32 times.
All inputs are finite; a program needn't handle non-finite values.
Results may differ from a plain program's by a relative error of at most 0.0003.
Values sent between devices are 32-bit elements; how exact they have to be, the bound alone decides.
A program may use at most 256 MiB of HBM per device.

v0:
```python
import functools

import jax
import jax.numpy as jnp
from jax import lax
from jax.experimental import pallas as pl
from jax.experimental.pallas import tpu as pltpu
from jax.sharding import PartitionSpec as P

SWEEPS = 4
EPSILON = 1e-06
LOW = 16
MESH = pl.DeviceIdType.MESH
F32 = jnp.float32
BF16 = jnp.bfloat16
PAIRS = [(i, j) for j in range(1, SWEEPS + 1) for i in range(j + 1)]
WIDTH = SWEEPS


def lookup_kernel(omega_ref, sigma_ref, ids_ref, damping_ref):
    planes, rows, lanes = ids_ref.shape
    tables = [jnp.broadcast_to(sigma_ref[k : k + 1, :], (8, lanes)) for k in range(sigma_ref.shape[0])]
    omega = omega_ref[0]
    per = rows // 8

    def step(i, carry):
        x, y = i // per, pl.multiple_of(i % per * 8, 8)
        ids = ids_ref[x, pl.ds(y, 8), :]
        low, high = ids & (lanes - 1), ids >> 7
        value = jnp.take_along_axis(tables[0], low, axis=1)
        for k in range(1, len(tables)):
            value = jnp.where(high == k, jnp.take_along_axis(tables[k], low, axis=1), value)
        damping_ref[x, pl.ds(y, 8), :] = omega * value
        return carry

    lax.fori_loop(0, planes * per, step, 0, unroll=8)


def split(values):
    high = values.astype(BF16)
    return high, (values - high.astype(F32)).astype(BF16)


def kernel(
    n, nf, high_blocks,
    omega_ref, source_ref, damping_ref, ids_ref, owner_ref, edge_ref, observed_ref,
    forward_ref, adjoint_ref, gradient_ref,
    real_ref, imag_ref, beside, pack_ref, mis_out, mis_in,
    basis, zb, curl, up_out, down_out, low_in, high_in,
    gram_out, gram_in, pack_in, grad_out, grad_in, grad_out2, grad_in2,
    rows_hot, rows_hot_t, field_hi, field_lo, mis_hi, mis_lo, acc,
    up_s, up_r, down_s, down_r, gram_s, gram_r, pack_s, pack_r, grad_s, grad_r, grad2_s, grad2_r,
    near_s, near_r,
):
    me = lax.axis_index("slab")
    mine = lax.axis_index("freq")
    planes, rows, lanes = damping_ref.shape
    first, last = WIDTH, WIDTH + planes - 1
    wide_planes = planes + 2 * WIDTH
    cells_rows = 3 * planes * rows
    wide_rows = 3 * wide_planes * rows

    barrier = pltpu.get_barrier_semaphore()
    for d in range(1, n):
        pl.semaphore_signal(barrier, inc=1, device_id={"slab": lax.rem(me + d, n)}, device_id_type=MESH)
    for d in range(1, nf):
        pl.semaphore_signal(barrier, inc=1, device_id={"freq": lax.rem(mine + d, nf)}, device_id_type=MESH)
    pl.semaphore_wait(barrier, n + nf - 2)

    def spread(src, dst, send, recv, axis, count, position):
        copies = []
        for d in range(1, count):
            copy = pltpu.make_async_remote_copy(
                src_ref=src, dst_ref=dst.at[d], send_sem=send.at[d], recv_sem=recv.at[d],
                device_id={axis: lax.rem(position + d, count)}, device_id_type=MESH,
            )
            copy.start()
            copies.append(copy)
        return copies

    def total_of(own, buffer, count, position):
        buffer[0] = own
        total = jnp.zeros(own.shape, F32)
        for p in range(count):
            total = total + buffer[lax.rem(position - p + count, count)]
        return total

    lane = lax.broadcasted_iota(jnp.int32, (rows, lanes), 1)
    row = lax.broadcasted_iota(jnp.int32, (rows, lanes), 0)

    def f3(v):
        return jnp.where(lane == lanes - 1, 0.0, pltpu.roll(v, lanes - 1, 1)) - v

    def g3(v):
        return jnp.where(lane == 0, 0.0, pltpu.roll(v, 1, 1)) - v

    def f2(v):
        return jnp.where(row == rows - 1, 0.0, pltpu.roll(v, rows - 1, 0)) - v

    def g2(v):
        return jnp.where(row == 0, 0.0, pltpu.roll(v, 1, 0)) - v

    edge = edge_ref[...]
    blank = jnp.zeros((3, lanes), F32)
    pack_ref[...] = jnp.concatenate(
        [owner_ref[...].astype(F32), (edge >> 7).astype(F32), (edge & 127).astype(F32), observed_ref[...], blank],
        axis=0,
    )
    packs = []
    for d in range(1, n):
        copy = pltpu.make_async_remote_copy(
            src_ref=pack_ref, dst_ref=pack_in.at[me], send_sem=pack_s.at[d], recv_sem=pack_r.at[d],
            device_id={"slab": lax.rem(me + d, n)}, device_id_type=MESH,
        )
        copy.start()
        packs.append(copy)
    pack_in[me] = pack_ref[...]
    valid = jnp.where(me > 0, 1.0, 0.0).astype(F32)

    def factors(x, damping):
        inverse = 1.0 / (16.0 + damping * damping)
        real_ref[x] = 4.0 * inverse
        imag_ref[x] = damping * inverse

    def own_factors(x, carry):
        factors(x + first, damping_ref[x])
        for c in range(2):
            for comp in range(3):
                basis[0, c, comp, x + first] = source_ref[c, comp, x].astype(F32)
        return carry

    lax.fori_loop(0, planes, own_factors, 0)

    def beside_copy(side):
        begin, to = (planes - WIDTH, me + 1) if side == 0 else (0, me + n - 1)
        return pltpu.make_async_remote_copy(
            src_ref=damping_ref.at[pl.ds(begin, WIDTH)], dst_ref=beside.at[side], send_sem=near_s.at[side],
            recv_sem=near_r.at[side], device_id={"slab": lax.rem(to, n)}, device_id_type=MESH,
        )

    def misfit_copy(side):
        to = me + 1 if side == 0 else me + n - 1
        return pltpu.make_async_remote_copy(
            src_ref=mis_out, dst_ref=mis_in.at[side], send_sem=near_s.at[2 + side],
            recv_sem=near_r.at[2 + side], device_id={"slab": lax.rem(to, n)}, device_id_type=MESH,
        )

    def precondition(t, x):
        mr, mi = real_ref[x], imag_ref[x]
        for comp in range(3):
            br, bi = basis[t, 0, comp, x], basis[t, 1, comp, x]
            zb[0, comp, x] = mr * br + mi * bi
            zb[1, comp, x] = mr * bi - mi * br

    def up_copy(slot):
        return pltpu.make_async_remote_copy(
            src_ref=up_out.at[slot], dst_ref=low_in.at[slot], send_sem=up_s.at[slot],
            recv_sem=up_r.at[slot], device_id={"slab": lax.rem(me + 1, n)}, device_id_type=MESH,
        )

    def down_copy(slot):
        return pltpu.make_async_remote_copy(
            src_ref=down_out.at[slot], dst_ref=high_in.at[slot], send_sem=down_s.at[slot],
            recv_sem=down_r.at[slot], device_id={"slab": lax.rem(me + n - 1, n)}, device_id_type=MESH,
        )

    def plane(t, c, x, e2n, e3n, b2p, b3p):
        e1, e2, e3 = zb[c, 0, x], zb[c, 1, x], zb[c, 2, x]
        b1 = f2(e3) - f3(e2)
        b2 = f3(e1) - (e3n - e3)
        b3 = e2n - e2 - f2(e1)
        curl[c, 0, x], curl[c, 1, x] = b2, b3
        basis[t + 1, c, 0, x] = g3(b2) - g2(b3) - 4.0 * e1 + basis[t, c, 0, x]
        basis[t + 1, c, 1, x] = b3p - b3 - g3(b1) - 4.0 * e2 + basis[t, c, 1, x]
        basis[t + 1, c, 2, x] = g2(b1) - (b2p - b2) - 4.0 * e3 + basis[t, c, 2, x]

    def lower_curl(x):
        for c in range(2):
            curl[c, 0, x] = f3(zb[c, 0, x]) - (zb[c, 2, x + 1] - zb[c, 2, x])
            curl[c, 1, x] = zb[c, 1, x + 1] - zb[c, 1, x] - f2(zb[c, 0, x])

    def apply(t, meanwhile):
        slot = t
        precondition(t, first)
        for c in range(2):
            down_out[slot, c, 0] = zb[c, 1, first]
            down_out[slot, c, 1] = zb[c, 2, first]

        @pl.when(me > 0)
        def _():
            down_copy(slot).start()

        precondition(t, last)
        for c in range(2):
            up_out[slot, c, 0] = f3(zb[c, 0, last]) + zb[c, 2, last]
            up_out[slot, c, 1] = f2(zb[c, 0, last]) + zb[c, 1, last]

        @pl.when(me < n - 1)
        def _():
            up_copy(slot).start()

        def inner(x, carry):
            precondition(t, x)
            return carry

        lax.fori_loop(first + 1, last, inner, 0)
        lower_curl(first)

        def middle(x, carry):
            for c in range(2):
                plane(t, c, x, zb[c, 1, x + 1], zb[c, 2, x + 1], curl[c, 0, x - 1], curl[c, 1, x - 1])
            return carry

        lax.fori_loop(first + 1, last, middle, 0)
        meanwhile()

        @pl.when(me > 0)
        def _():
            up_copy(slot).wait_recv()
            down_copy(slot).wait_send()

        @pl.when(me == 0)
        def _():
            low_in[slot] = jnp.zeros(low_in.shape[1:], F32)

        for c in range(2):
            plane(
                t, c, first, zb[c, 1, first + 1], zb[c, 2, first + 1],
                (low_in[slot, c, 0] - zb[c, 2, first]) * valid,
                (zb[c, 1, first] - low_in[slot, c, 1]) * valid,
            )

        @pl.when(me < n - 1)
        def _():
            down_copy(slot).wait_recv()
            up_copy(slot).wait_send()

        @pl.when(me == n - 1)
        def _():
            high_in[slot] = jnp.zeros(high_in.shape[1:], F32)

        for c in range(2):
            plane(
                t, c, last, high_in[slot, c, 0], high_in[slot, c, 1],
                curl[c, 0, last - 1], curl[c, 1, last - 1],
            )

    def apply_wide(t):
        def inner(x, carry):
            precondition(t, x)
            return carry

        lax.fori_loop(t, wide_planes - t, inner, 0)
        lower_curl(t)

        def middle(x, carry):
            keep = jnp.where((x == first) & (me == 0), 0.0, 1.0).astype(F32)
            for c in range(2):
                plane(
                    t, c, x, zb[c, 1, x + 1], zb[c, 2, x + 1],
                    curl[c, 0, x - 1] * keep, curl[c, 1, x - 1] * keep,
                )
            return carry

        lax.fori_loop(t + 1, wide_planes - t - 1, middle, 0)

    per = rows // 8

    def solve(which, out_ref):
        def pair_sums(j_):
            width = 2 * j_ + 1

            def products(i, sums):
                x, y = i // per + first, pl.multiple_of(i % per * 8, 8)
                sums = list(sums)
                for comp in range(3):
                    re = [basis[k, 0, comp, x, pl.ds(y, 8), :] for k in range(j_ + 1)]
                    im = [basis[k, 1, comp, x, pl.ds(y, 8), :] for k in range(j_ + 1)]
                    for i_ in range(j_ + 1):
                        sums[2 * i_] = sums[2 * i_] + (re[i_] * re[j_] + im[i_] * im[j_])
                        if i_ != j_:
                            sums[2 * i_ + 1] = sums[2 * i_ + 1] + (re[i_] * im[j_] - im[i_] * re[j_])
                return tuple(sums)

            zero = jnp.zeros((8, lanes), F32)
            sums = lax.fori_loop(0, planes * per, products, (zero,) * width, unroll=2)
            for k in range(width):
                at = j_ * j_ - 1 + k
                gram_out[which, at : at + 1, :] = jnp.sum(sums[k], axis=0, keepdims=True)

        for t in range(SWEEPS):
            if which == 0:
                apply(t, functools.partial(pair_sums, t) if t else lambda: None)
            else:
                apply_wide(t)
                if t:
                    pair_sums(t)
        pair_sums(SWEEPS)
        copies = spread(gram_out.at[which], gram_in.at[which], gram_s.at[which], gram_r.at[which], "slab", n, me)
        for copy in copies:
            copy.wait()
        if which == 0:
            @pl.when(me > 0)
            def _():
                beside_copy(1).start()

            @pl.when(me < n - 1)
            def _():
                beside_copy(0).start()
        total = total_of(gram_out[which], gram_in.at[which], n, me)
        total = jnp.broadcast_to(jnp.sum(total, axis=1, keepdims=True), total.shape)
        gram, at = {}, 0
        for i, j in PAIRS:
            re = total[at : at + 1, :]
            at += 1
            im = jnp.zeros_like(re)
            if i != j:
                im = total[at : at + 1, :]
                at += 1
            gram[i, j] = (re, im)
            gram[j, i] = (re, -im)
        one = jnp.ones((1, lanes), F32)
        none = jnp.zeros((1, lanes), F32)

        def times(a, b):
            return a[0] * b[0] - a[1] * b[1], a[0] * b[1] + a[1] * b[0]

        poly = [(one, none)]
        coef = [(none, none) for _ in range(SWEEPS)]
        for k in range(SWEEPS):
            up = (none, none)
            below = none
            for i in range(k + 1):
                conj = (poly[i][0], -poly[i][1])
                for j in range(k + 1):
                    both = times(conj, poly[j])
                    term = times(both, gram[i + 1, j])
                    up = (up[0] + term[0], up[1] + term[1])
                    below = below + times(both, gram[i + 1, j + 1])[0]
            below = below + EPSILON
            step = (up[0] / below, up[1] / below)
            moved = [times(step, p) for p in poly]
            for i in range(k + 1):
                coef[i] = (coef[i][0] + moved[i][0], coef[i][1] + moved[i][1])
            grown = poly + [(none, none)]
            for i in range(k + 1):
                grown[i + 1] = (grown[i + 1][0] - moved[i][0], grown[i + 1][1] - moved[i][1])
            poly = grown

        wide = [(jnp.broadcast_to(a, (rows, lanes)), jnp.broadcast_to(b, (rows, lanes))) for a, b in coef]

        def combine(x, carry):
            mr, mi = real_ref[x + first], imag_ref[x + first]
            for comp in range(3):
                sr = jnp.zeros((rows, lanes), F32)
                si = jnp.zeros((rows, lanes), F32)
                for k in range(SWEEPS):
                    br, bi = basis[k, 0, comp, x + first], basis[k, 1, comp, x + first]
                    sr = sr + (wide[k][0] * br - wide[k][1] * bi)
                    si = si + (wide[k][0] * bi + wide[k][1] * br)
                out_ref[0, comp, x] = mr * sr + mi * si
                out_ref[1, comp, x] = mr * si - mi * sr
            return carry

        lax.fori_loop(0, planes, combine, 0)

    solve(0, forward_ref)

    for copy in packs:
        copy.wait()
    self_id = me.astype(F32)
    blocks = cells_rows // lanes
    wide_blocks = wide_rows // lanes
    for comp in range(3):
        for c in range(2):
            hi, lo = split(forward_ref[c, comp].reshape(planes * rows, lanes))
            where = (slice(comp * planes * rows, (comp + 1) * planes * rows), slice(c * lanes, (c + 1) * lanes))
            field_hi[where] = hi
            field_lo[where] = lo

    lane_sq = lax.broadcasted_iota(jnp.int32, (lanes, lanes), 1).astype(F32)
    row_sq = lax.broadcasted_iota(jnp.int32, (lanes, lanes), 0).astype(F32)

    def receivers(d, carry):
        pack = pack_in[d]
        at = pl.ds(pl.multiple_of(d * lanes, lanes), lanes)
        owned = jnp.where(pack[0:1, :] == self_id, pack[1:2, :], -1.0)
        owned = jnp.concatenate([owned, pack[2:8, :], owned], axis=0)
        column = jnp.concatenate([owned] * (lanes // 8), axis=0).T
        place = column[:, 0:1]
        for k in range(blocks):
            rows_hot[:, k * lanes : (k + 1) * lanes] = jnp.where(
                lane_sq == place - float(k * lanes), 1.0, 0.0
            ).astype(BF16)
        picked = jnp.dot(rows_hot[...], field_hi[...], preferred_element_type=F32)
        picked = picked + jnp.dot(rows_hot[...], field_lo[...], preferred_element_type=F32)
        here = (lane_sq == column[:, 1:2]) & (place >= 0.0)
        re = jnp.where(here, picked[:, :lanes] - column[:, 2:3], 0.0)
        im = jnp.where(here, column[:, 3:4] - picked[:, lanes:], 0.0)
        both = jnp.where(
            lane_sq == 0.0,
            jnp.sum(re, axis=1, keepdims=True),
            jnp.where(lane_sq == 1.0, jnp.sum(im, axis=1, keepdims=True), 0.0),
        )
        mis_out[d] = both.T[0:8, :]
        return carry

    lax.fori_loop(0, n, receivers, 0)

    @pl.when(me > 0)
    def _():
        misfit_copy(1).start()

    @pl.when(me < n - 1)
    def _():
        misfit_copy(0).start()

    def places(p, carry):
        at = pl.ds(pl.multiple_of(p * lanes, lanes), lanes)
        pack = pack_in[p]
        apart = pack[0:1, :] - self_id
        number = pack[1:2, :].astype(jnp.int32)
        comp = jnp.where(number >= 2 * planes * rows, 2, jnp.where(number >= planes * rows, 1, 0))
        offset = (apart * float(planes * rows)).astype(jnp.int32) + WIDTH * rows
        inside = number - comp * (planes * rows) + offset
        fits = (inside >= 0) & (inside < wide_planes * rows)
        spot = jnp.where(fits, inside + comp * (wide_planes * rows), -1).astype(F32)
        for k in range(wide_blocks):
            rows_hot_t[k * lanes : (k + 1) * lanes, at] = jnp.where(
                row_sq == spot - float(k * lanes), 1.0, 0.0
            ).astype(BF16)
        return carry

    lax.fori_loop(0, n, places, 0)

    @pl.when(me > 0)
    def _():
        misfit_copy(0).wait_recv()
        misfit_copy(1).wait_send()
        beside_copy(0).wait_recv()
        beside_copy(1).wait_send()

    @pl.when(me < n - 1)
    def _():
        misfit_copy(1).wait_recv()
        misfit_copy(0).wait_send()
        beside_copy(1).wait_recv()
        beside_copy(0).wait_send()

    for side, there in enumerate((me > 0, me < n - 1)):
        start = 0 if side == 0 else last + 1

        @pl.when(there)
        def _(side=side, start=start):
            for k in range(WIDTH):
                factors(start + k, beside[side, k])

        @pl.when(jnp.logical_not(there))
        def _(side=side, start=start):
            mis_in[side] = jnp.zeros(mis_in.shape[1:], F32)
            for k in range(WIDTH):
                real_ref[start + k] = jnp.zeros((rows, lanes), F32)
                imag_ref[start + k] = jnp.zeros((rows, lanes), F32)

    def values_of(p, carry):
        at = pl.ds(pl.multiple_of(p * lanes, lanes), lanes)
        value = mis_out[p] + mis_in[0, p] + mis_in[1, p]
        value = jnp.concatenate([value[0:2, :], pack_in[p][2:8, :]], axis=0)
        column = jnp.concatenate([value] * (lanes // 8), axis=0).T
        here = lane_sq == column[:, 2:3]
        for part in range(2):
            hi, lo = split(jnp.where(here, column[:, part : part + 1], 0.0))
            mis_hi[at, part * lanes : (part + 1) * lanes] = hi
            mis_lo[at, part * lanes : (part + 1) * lanes] = lo
        return carry

    lax.fori_loop(0, n, values_of, 0)
    group = 4
    for comp in range(3):
        for x in range(0, wide_planes, group):
            begin = (comp * wide_planes + x) * rows
            hot = rows_hot_t[begin : begin + group * rows, :]
            added = jnp.dot(hot, mis_hi[...], preferred_element_type=F32)
            added = added + jnp.dot(hot, mis_lo[...], preferred_element_type=F32)
            for c in range(2):
                basis[0, c, comp, x : x + group] = added[:, c * lanes : (c + 1) * lanes].reshape(
                    group, rows, lanes
                )

    solve(1, adjoint_ref)

    omega = omega_ref[0]
    high_iota = lax.broadcasted_iota(jnp.int32, (high_blocks, lanes), 0)
    low_iota = lax.broadcasted_iota(jnp.int32, (LOW, lanes), 0)
    acc[...] = jnp.zeros(acc.shape, F32)
    chunks = rows // 16

    def cells(i, carry):
        x, y = i // chunks, pl.multiple_of(i % chunks * 16, 16)
        value = jnp.zeros((16, lanes), F32)
        for comp in range(3):
            fr, fi = forward_ref[0, comp, x, pl.ds(y, 16), :], forward_ref[1, comp, x, pl.ds(y, 16), :]
            ar, ai = adjoint_ref[0, comp, x, pl.ds(y, 16), :], adjoint_ref[1, comp, x, pl.ds(y, 16), :]
            value = value + (ar * fi + ai * fr)
        value = omega * value
        ids = ids_ref[x, pl.ds(y, 16), :]
        high, low = ids >> 4, ids & (LOW - 1)
        hot = jnp.concatenate(
            [jnp.where(high[r : r + 1, :] == high_iota, 1.0, 0.0) for r in range(16)], axis=0
        ).astype(BF16)
        spot = jnp.concatenate(
            [jnp.where(low[r : r + 1, :] == low_iota, value[r : r + 1, :], 0.0) for r in range(16)], axis=0
        )
        acc[...] += lax.dot_general(
            jnp.concatenate([hot, hot], axis=1), jnp.concatenate(split(spot), axis=1),
            (((1,), (1,)), ((), ())), preferred_element_type=F32,
        )
        return carry

    lax.fori_loop(0, planes * chunks, cells, 0, unroll=4)
    wide_lane = lax.broadcasted_iota(jnp.int32, (high_blocks, 16 * LOW), 1)
    diagonal = jnp.zeros((high_blocks, 16 * LOW), F32)
    for r in range(16):
        inside = (wide_lane >= r * LOW) & (wide_lane < (r + 1) * LOW)
        diagonal = diagonal + jnp.where(inside, acc[r * high_blocks : (r + 1) * high_blocks, :], 0.0)
    folded = diagonal[:, :lanes] + diagonal[:, lanes:]
    for shift in (64, 32, 16):
        folded = folded + pltpu.roll(folded, shift, 1)
    grad_out[...] = folded
    for copy in spread(grad_out, grad_in, grad_s, grad_r, "slab", n, me):
        copy.wait()
    partial = total_of(grad_out[...], grad_in, n, me)
    grad_out2[...] = partial
    for copy in spread(grad_out2, grad_in2, grad2_s, grad2_r, "freq", nf, mine):
        copy.wait()
    gradient_ref[...] = total_of(partial, grad_in2, nf, mine)


def body(source, omega, sigma_blocks, block_ids, rec_owner, rec_edge, observed):
    n, nf = lax.axis_size("slab"), lax.axis_size("freq")
    planes, rows, lanes = block_ids.shape
    blocks = sigma_blocks.shape[0]
    high_blocks = blocks // LOW
    vmem = pl.BlockSpec(memory_space=pltpu.VMEM)
    smem = pl.BlockSpec(memory_space=pltpu.SMEM)
    cell = jax.ShapeDtypeStruct((planes, rows, lanes), F32)
    damping = pl.pallas_call(
        lookup_kernel,
        out_shape=cell,
        in_specs=[smem, vmem, vmem],
        out_specs=vmem,
        name="lookup",
    )(omega, sigma_blocks.reshape(-1, lanes), block_ids)
    count = sum(1 if i == j else 2 for i, j in PAIRS)
    slots = SWEEPS
    cells_rows = 3 * planes * rows
    wide_planes = planes + 2 * WIDTH
    field = jax.ShapeDtypeStruct((2, 3, planes, rows, lanes), F32)
    halo = pltpu.VMEM((slots, 2, 2, rows, lanes), F32)
    dma = pltpu.SemaphoreType.DMA
    grad = pltpu.VMEM((high_blocks, lanes), F32)
    forward, adjoint, gradient = pl.pallas_call(
        functools.partial(kernel, n, nf, high_blocks),
        out_shape=(field, field, jax.ShapeDtypeStruct((high_blocks, lanes), F32)),
        in_specs=[smem] + [pl.BlockSpec()] * 6,
        out_specs=(vmem, vmem, vmem),
        scratch_shapes=[
            pltpu.VMEM((wide_planes, rows, lanes), F32),
            pltpu.VMEM((wide_planes, rows, lanes), F32),
            pltpu.VMEM((2, WIDTH, rows, lanes), F32),
            pltpu.VMEM((8, lanes), F32),
            pltpu.VMEM((n, 8, lanes), F32),
            pltpu.VMEM((2, n, 8, lanes), F32),
            pltpu.VMEM((SWEEPS + 1, 2, 3, wide_planes, rows, lanes), F32),
            pltpu.VMEM((2, 3, wide_planes, rows, lanes), F32),
            pltpu.VMEM((2, 2, wide_planes, rows, lanes), F32),
            halo, halo, halo, halo,
            pltpu.VMEM((2, count, lanes), F32),
            pltpu.VMEM((2, n, count, lanes), F32),
            pltpu.VMEM((n, 8, lanes), F32),
            grad,
            pltpu.VMEM((n, high_blocks, lanes), F32),
            grad,
            pltpu.VMEM((nf, high_blocks, lanes), F32),
            pltpu.VMEM((lanes, cells_rows), BF16),
            pltpu.VMEM((3 * wide_planes * rows, n * lanes), BF16),
            pltpu.VMEM((cells_rows, 2 * lanes), BF16),
            pltpu.VMEM((cells_rows, 2 * lanes), BF16),
            pltpu.VMEM((n * lanes, 2 * lanes), BF16),
            pltpu.VMEM((n * lanes, 2 * lanes), BF16),
            pltpu.VMEM((16 * high_blocks, 16 * LOW), F32),
            dma((slots,)), dma((slots,)), dma((slots,)), dma((slots,)),
            dma((2, n)), dma((2, n)),
            dma((n,)), dma((n,)),
            dma((n,)), dma((n,)),
            dma((nf,)), dma((nf,)),
            dma((4,)), dma((4,)),
        ],
        compiler_params=pltpu.CompilerParams(
            collective_id=0, has_side_effects=True, vmem_limit_bytes=52 * 1024 * 1024
        ),
        name="solves",
    )(
        omega, source[0], damping, block_ids,
        rec_owner.reshape(1, -1), rec_edge.reshape(1, -1), observed[0],
    )
    return forward[None], adjoint[None], gradient[:, :LOW].reshape(blocks)


def solution(mesh):
    return jax.shard_map(
        body,
        mesh=mesh,
        in_specs=(
            P("freq", None, None, "slab", None, None),
            P("freq"),
            P(),
            P("slab", None, None),
            P("slab", None),
            P("slab"),
            P("freq", None, "slab"),
        ),
        out_specs=(
            P("freq", None, None, "slab", None, None),
            P("freq", None, None, "slab", None, None),
            P(),
        ),
        check_vma=False,
    )
```

profile of v0, /device:TPU:0, one launch (start us, length us, event | category | flops | bytes accessed | tf_op | source)
XLA Modules:
  0.0 104.0 jit_solution(16471772674599110872)
XLA Ops:
  1.3 2.6 %lookup.1.damping_ref = f32[8,64,128]{2,1,0:T(8,128)} custom-call(f32[1]{0:T(128)S(6)} %copy.12.omega_ref, f32[2,128]{1,0:T(2,128)} %bitcast.15, s32[8,64,128]{2,1,0:T(8,128)} %ids_ref.3), custom_call_target="tpu_custom_call" | custom-call | tf_op jit(solution)/shard_map/lookup/pallas_call | solution.py:547
  3.9 0.0 copy-start
  3.9 0.9 copy-done
  4.9 0.0 copy-start.1
  4.9 0.9 copy-done.1
  5.8 0.0 copy-start.2
  5.8 1.1 %copy-done.2 = bf16[1,2,3,8,64,128]{5,4,3,2,1,0:T(8,128)(2,1)S(1)} copy-done((bf16[1,2,3,8,64,128]{5,4,3,2,1,0:T(8,128)(2,1)S(1)}, bf16[1,2,3,8,64,128]{5,4,3,2,1,0:T(8,128)(2,1)}, u32[]{:S(2)}) %copy-start.2) | copy-done | bytes 786456
  6.9 0.0 copy-start.3
  6.9 0.7 copy-done.3
  7.6 0.0 copy-start.4
  7.6 0.7 copy-done.4
  8.3 0.0 copy-start.5
  8.3 0.7 copy-done.5
  8.9 90.4 %solves.1 = (f32[2,3,8,64,128]{4,3,2,1,0:T(8,128)}, f32[2,3,8,64,128]{4,3,2,1,0:T(8,128)}, f32[16,128]{1,0:T(8,128)S(1)}) custom-call(f32[1]{0:T(128)S(6)} %copy.12.omega_ref, bf16[2,3,8,64,128]{4,3,2,1,0:T(8,128)(2,1)S(1)} %bitcast.8, f32[8,64,128]{2,1,0:T(8,128)S(1)} %copy-done.1, s32[8,64,128]{2,1,0:T(8,128)S(1)} %copy-done, s32[1,128]{1,0:T(1,128)S(1)} %bitcast.11, ...), custom_call_target="tpu_custom_call" | custom-call | tf_op jit(solution)/shard_map/solves/pallas_call | solution.py:562
  99.4 0.6 reshape.21
  100.0 0.0 copy-start.6
  100.0 2.8 %copy.13 = f32[1,2,3,8,64,128]{5,4,3,2,1,0:T(8,128)} copy(f32[1,2,3,8,64,128]{5,4,3,2,1,0:T(8,128)} %bitcast.14) | data formatting | bytes 3145728
  102.8 0.0 copy-done.6
  102.8 1.1 %copy.14 = f32[1,2,3,8,64,128]{5,4,3,2,1,0:T(8,128)} copy(f32[1,2,3,8,64,128]{5,4,3,2,1,0:T(8,128)S(1)} %bitcast.13) | data formatting | bytes 3145728
Async XLA Ops:
  3.9 0.9 copy-start
  4.9 0.9 copy-start.1
  5.8 1.1 %copy-start.2 = (bf16[1,2,3,8,64,128]{5,4,3,2,1,0:T(8,128)(2,1)S(1)}, bf16[1,2,3,8,64,128]{5,4,3,2,1,0:T(8,128)(2,1)}, u32[]{:S(2)}) copy-start(bf16[1,2,3,8,64,128]{5,4,3,2,1,0:T(8,128)(2,1)} %param.7) | copy-start | bytes 2359300
  6.9 0.7 copy-start.3
  7.6 0.7 copy-start.4
  8.3 0.7 copy-start.5
  100.0 2.9 %copy-start.6 = (f32[2,3,8,64,128]{4,3,2,1,0:T(8,128)S(1)}, f32[2,3,8,64,128]{4,3,2,1,0:T(8,128)}, u32[]{:S(2)}) copy-start(f32[2,3,8,64,128]{4,3,2,1,0:T(8,128)} %get-tuple-element.7) | copy-start | bytes 4718596
where the time goes:
time: 104 us
  Pallas kernels  93 us (89%)
  local copies, waits for them, and re-layouts  9.65 us (9%)
  between operations  1.29 us (1%)
    pallas_call x1, Pallas kernels, body(): pl.pallas_call(functools.partial(kernel, n, nf, high_blocks), out_shape=(...  90.4 us
    unnamed x16, local copies, waits for them, and re-layouts  9.01 us
    pallas_call x1, Pallas kernels, body(): pl.pallas_call(lookup_kernel, out_shape=cell, in_specs=[smem, vmem, vmem]...  2.63 us

commit v1 on v0

v1 whole, which is shorter than its diff:
```python
import functools

import jax
import jax.numpy as jnp
from jax import lax
from jax.experimental import pallas as pl
from jax.experimental.pallas import tpu as pltpu
from jax.sharding import PartitionSpec as P

SWEEPS = 4
EPSILON = 1e-06
LOW = 16
CAP = 32
MESH = pl.DeviceIdType.MESH
F32 = jnp.float32
BF16 = jnp.bfloat16
PAIRS = [(i, j) for j in range(1, SWEEPS + 1) for i in range(j + 1)]
COUNT = sum(1 if i == j else 2 for i, j in PAIRS)
WIDTH = SWEEPS


def split(values):
    high = values.astype(BF16)
    return high, (values - high.astype(F32)).astype(BF16)


def kernel(
    n, nf, high_blocks,
    omega_ref, source_hbm, sigma_hbm, ids_hbm, owner_hbm, edge_hbm, observed_hbm,
    forward_ref, adjoint_ref, gradient_ref,
    source_ref, sigma_ref, ids_ref, owner_ref, edge_ref, observed_ref,
    damp, real_ref, imag_ref, cond, beside, pack_ref, mis_out, mis_in,
    basis, zb, curl, up_out, down_out, low_in, high_in,
    gram_acc, gram_out, gram_in, pack_in, grad_out, grad_in, grad_out2, grad_in2,
    columns, hot, hot_t, field_hi, field_lo, mis_hi, mis_lo, acc,
    local_s, up_s, up_r, down_s, down_r, gram_s, gram_r, pack_s, pack_r, grad_s, grad_r, grad2_s, grad2_r,
    near_s, near_r, share_s, share_r,
):
    me = lax.axis_index("slab")
    mine = lax.axis_index("freq")
    planes, rows, lanes = ids_ref.shape
    first, last = WIDTH, WIDTH + planes - 1
    wide_planes = planes + 2 * WIDTH
    cells_rows = 3 * planes * rows
    slots = n * CAP
    side_rows = WIDTH * rows
    part = side_rows // nf

    loads = [
        pltpu.make_async_copy(src, dst, local_s.at[k])
        for k, (src, dst) in enumerate([
            (ids_hbm, ids_ref), (sigma_hbm, sigma_ref), (source_hbm, source_ref),
            (owner_hbm, owner_ref), (edge_hbm, edge_ref), (observed_hbm, observed_ref),
        ])
    ]
    for copy in loads:
        copy.start()

    barrier = pltpu.get_barrier_semaphore()
    for d in range(1, n):
        pl.semaphore_signal(barrier, inc=1, device_id={"slab": lax.rem(me + d, n)}, device_id_type=MESH)
    for d in range(1, nf):
        pl.semaphore_signal(barrier, inc=1, device_id={"freq": lax.rem(mine + d, nf)}, device_id_type=MESH)

    def spread(src, dst, send, recv, axis, count, position):
        copies = []
        for d in range(1, count):
            copy = pltpu.make_async_remote_copy(
                src_ref=src, dst_ref=dst.at[d], send_sem=send.at[d], recv_sem=recv.at[d],
                device_id={axis: lax.rem(position + d, count)}, device_id_type=MESH,
            )
            copy.start()
            copies.append(copy)
        return copies

    def total_of(own, buffer, count, position):
        buffer[0] = own
        total = jnp.zeros(own.shape, F32)
        for p in range(count):
            total = total + buffer[lax.rem(position - p + count, count)]
        return total

    lane = lax.broadcasted_iota(jnp.int32, (rows, lanes), 1)
    row = lax.broadcasted_iota(jnp.int32, (rows, lanes), 0)
    inner = slice(0, rows)
    above = slice(1, rows + 1)
    shifted = slice(8, rows + 8)
    under = slice(7, rows + 7)

    def f3(v):
        return jnp.where(lane == lanes - 1, 0.0, pltpu.roll(v, lanes - 1, 1)) - v

    def g3(v):
        return jnp.where(lane == 0, 0.0, pltpu.roll(v, 1, 1)) - v

    valid = jnp.where(me > 0, 1.0, 0.0).astype(F32)
    omega = omega_ref[0]

    def factors(x, at, damping):
        inverse = 1.0 / (16.0 + damping * damping)
        damp[x, at] = damping
        real_ref[x, at] = 4.0 * inverse
        imag_ref[x, at] = damping * inverse

    def pad(x, carry):
        for c in range(2):
            for comp in range(3):
                zb[c, comp, x, rows : rows + 8] = jnp.zeros((8, lanes), F32)
                curl[c, comp, x, 0:8] = jnp.zeros((8, lanes), F32)
        return carry

    lax.fori_loop(0, wide_planes, pad, 0)

    chunks = rows // 16
    loads[0].wait()
    loads[1].wait()
    loads[2].wait()
    tables = [jnp.broadcast_to(sigma_ref[k : k + 1, :], (8, lanes)) for k in range(sigma_ref.shape[0])]

    def begin(x, y):
        for half in range(2):
            at = pl.ds(pl.multiple_of(y + 8 * half, 8), 8)
            ids = ids_ref[x, at, :]
            low, high = ids & (lanes - 1), ids >> 7
            value = jnp.take_along_axis(tables[0], low, axis=1)
            for k in range(1, len(tables)):
                value = jnp.where(high == k, jnp.take_along_axis(tables[k], low, axis=1), value)
            cond[pl.ds(pl.multiple_of(x * rows + y + 8 * half, 8), 8), :] = value
            factors(x + first, at, omega * value)
        at = pl.ds(y, 16)
        for c in range(2):
            for comp in range(3):
                basis[0, c, comp, x + first, at] = source_ref[c, comp, x, at, :].astype(F32)

    def begin_ends(i, carry):
        begin(i // chunks * (planes - 1), pl.multiple_of(i % chunks * 16, 16))
        return carry

    def begin_inner(i, carry):
        begin(i // chunks + 1, pl.multiple_of(i % chunks * 16, 16))
        return carry

    lax.fori_loop(0, 2 * chunks, begin_ends, 0, unroll=4)

    def beside_copy(side):
        start, to = (planes * rows - side_rows, me + 1) if side == 0 else (0, me + n - 1)
        return pltpu.make_async_remote_copy(
            src_ref=cond.at[pl.ds(start + mine * part, part)], dst_ref=beside.at[side, pl.ds(mine * part, part)],
            send_sem=near_s.at[side], recv_sem=near_r.at[side], device_id={"slab": lax.rem(to, n)},
            device_id_type=MESH,
        )

    def share_copies(side):
        at = pl.ds(mine * part, part)
        return [
            pltpu.make_async_remote_copy(
                src_ref=beside.at[side, at], dst_ref=beside.at[side, at], send_sem=share_s.at[side, d],
                recv_sem=share_r.at[side, d], device_id={"freq": lax.rem(mine + d, nf)}, device_id_type=MESH,
            )
            for d in range(1, nf)
        ]

    def misfit_copy(side):
        to = me + 1 if side == 0 else me + n - 1
        return pltpu.make_async_remote_copy(
            src_ref=mis_out, dst_ref=mis_in.at[side], send_sem=near_s.at[2 + side],
            recv_sem=near_r.at[2 + side], device_id={"slab": lax.rem(to, n)}, device_id_type=MESH,
        )

    def up_copy(slot):
        return pltpu.make_async_remote_copy(
            src_ref=up_out.at[slot], dst_ref=low_in.at[slot], send_sem=up_s.at[slot],
            recv_sem=up_r.at[slot], device_id={"slab": lax.rem(me + 1, n)}, device_id_type=MESH,
        )

    def down_copy(slot):
        return pltpu.make_async_remote_copy(
            src_ref=down_out.at[slot], dst_ref=high_in.at[slot], send_sem=down_s.at[slot],
            recv_sem=down_r.at[slot], device_id={"slab": lax.rem(me + n - 1, n)}, device_id_type=MESH,
        )

    def precondition(t, x):
        mr, mi = real_ref[x], imag_ref[x]
        for comp in range(3):
            br, bi = basis[t, 0, comp, x], basis[t, 1, comp, x]
            zb[0, comp, x, inner] = mr * br + mi * bi
            zb[1, comp, x, inner] = mr * bi - mi * br

    def curls(x, ahead=None):
        for c in range(2):
            e1, e2, e3 = zb[c, 0, x, inner], zb[c, 1, x, inner], zb[c, 2, x, inner]
            if ahead is None:
                e2n, e3n = zb[c, 1, x + 1, inner], zb[c, 2, x + 1, inner]
            else:
                e2n, e3n = ahead[c, 0], ahead[c, 1]
            curl[c, 0, x, shifted] = (zb[c, 2, x, above] - e3) - f3(e2)
            curl[c, 1, x, shifted] = f3(e1) - (e3n - e3)
            curl[c, 2, x, shifted] = (e2n - e2) - (zb[c, 0, x, above] - e1)

    def images(t, x, keep=None):
        damping = damp[x]
        for c in range(2):
            b1, b2, b3 = curl[c, 0, x, shifted], curl[c, 1, x, shifted], curl[c, 2, x, shifted]
            b2p, b3p = curl[c, 1, x - 1, shifted], curl[c, 2, x - 1, shifted]
            if keep is not None:
                b2p, b3p = b2p * keep, b3p * keep
            parts = (
                g3(b2) - (curl[c, 2, x, under] - b3),
                (b3p - b3) - g3(b1),
                (curl[c, 0, x, under] - b1) - (b2p - b2),
            )
            for comp in range(3):
                turned = damping * zb[1 - c, comp, x, inner]
                basis[t + 1, c, comp, x] = parts[comp] - turned if c == 0 else parts[comp] + turned

    def sweep(t, lo, hi, masked):
        for k in range(4):
            precondition(t, lo + k)
        curls(lo)
        curls(lo + 1)

        def keep_of(x):
            if not masked:
                return None
            return jnp.where((x == first) & (me == 0), 0.0, 1.0).astype(F32)

        def step(x, carry):
            images(t, x, keep_of(x))
            curls(x + 1)
            precondition(t, x + 3)
            return carry

        lax.fori_loop(lo + 1, hi - 2, step, 0)
        images(t, hi - 2)
        curls(hi - 1)
        images(t, hi - 1)

    def send_down(t):
        precondition(t, first)
        for c in range(2):
            down_out[t, c, 0] = zb[c, 1, first, inner]
            down_out[t, c, 1] = zb[c, 2, first, inner]

        @pl.when(me > 0)
        def _():
            down_copy(t).start()

    def send_up(t):
        precondition(t, last)
        for c in range(2):
            e1 = zb[c, 0, last, inner]
            up_out[t, c, 0] = f3(e1) + zb[c, 2, last, inner]
            up_out[t, c, 1] = (zb[c, 0, last, above] - e1) + zb[c, 1, last, inner]

        @pl.when(me < n - 1)
        def _():
            up_copy(t).start()

    def forward_sweep(t, meanwhile):
        sweep(t, first, last, False)
        meanwhile()

        @pl.when(me > 0)
        def _():
            up_copy(t).wait_recv()
            down_copy(t).wait_send()

        @pl.when(me == 0)
        def _():
            low_in[t] = jnp.zeros(low_in.shape[1:], F32)

        for c in range(2):
            curl[c, 1, first - 1, shifted] = (low_in[t, c, 0] - zb[c, 2, first, inner]) * valid
            curl[c, 2, first - 1, shifted] = (zb[c, 1, first, inner] - low_in[t, c, 1]) * valid
        images(t, first)
        if t < SWEEPS - 1:
            send_down(t + 1)

        @pl.when(me < n - 1)
        def _():
            down_copy(t).wait_recv()
            up_copy(t).wait_send()

        @pl.when(me == n - 1)
        def _():
            high_in[t] = jnp.zeros(high_in.shape[1:], F32)

        curls(last, high_in.at[t])
        images(t, last)
        if t < SWEEPS - 1:
            send_up(t + 1)

    per = rows // 8

    def pair_sums(j_):
        width = 2 * j_ + 1

        def products(i, sums):
            x, y = i // per + first, pl.multiple_of(i % per * 8, 8)
            sums = list(sums)
            for comp in range(3):
                re = [basis[k, 0, comp, x, pl.ds(y, 8), :] for k in range(j_ + 1)]
                im = [basis[k, 1, comp, x, pl.ds(y, 8), :] for k in range(j_ + 1)]
                for i_ in range(j_ + 1):
                    sums[2 * i_] = sums[2 * i_] + (re[i_] * re[j_] + im[i_] * im[j_])
                    if i_ != j_:
                        sums[2 * i_ + 1] = sums[2 * i_ + 1] + (re[i_] * im[j_] - im[i_] * re[j_])
            return tuple(sums)

        zero = jnp.zeros((8, lanes), F32)
        sums = lax.fori_loop(0, planes * per, products, (zero,) * width, unroll=2)
        for k in range(width):
            at = j_ * j_ - 1 + k
            gram_acc[at : at + 1, :] = jnp.sum(sums[k], axis=0, keepdims=True)

    gram_lane = lax.broadcasted_iota(jnp.int32, (COUNT, lanes), 1)
    gram_row = lax.broadcasted_iota(jnp.int32, (COUNT, lanes), 0)
    diagonal_of = gram_lane == gram_row

    def gram_start(which):
        local = jnp.sum(gram_acc[...], axis=1, keepdims=True)
        gram_out[which] = jnp.sum(jnp.where(diagonal_of, local, 0.0), axis=0, keepdims=True)
        return spread(gram_out.at[which], gram_in.at[which], gram_s.at[which], gram_r.at[which], "slab", n, me)

    def coefficients(which):
        total = total_of(gram_out[which], gram_in.at[which], n, me)
        total = jnp.sum(jnp.where(diagonal_of, total, 0.0), axis=1, keepdims=True)
        total = jnp.broadcast_to(total, (COUNT, lanes))
        gram, at = {}, 0
        for i, j in PAIRS:
            re = total[at : at + 1, :]
            at += 1
            im = jnp.zeros_like(re)
            if i != j:
                im = total[at : at + 1, :]
                at += 1
            gram[i, j] = (re, im)
            gram[j, i] = (re, -im)
        one = jnp.ones((1, lanes), F32)
        none = jnp.zeros((1, lanes), F32)

        def times(a, b):
            return a[0] * b[0] - a[1] * b[1], a[0] * b[1] + a[1] * b[0]

        poly = [(one, none)]
        coef = [(none, none) for _ in range(SWEEPS)]
        for k in range(SWEEPS):
            up = (none, none)
            below = none
            for i in range(k + 1):
                conj = (poly[i][0], -poly[i][1])
                for j in range(k + 1):
                    both = times(conj, poly[j])
                    term = times(both, gram[i + 1, j])
                    up = (up[0] + term[0], up[1] + term[1])
                    below = below + times(both, gram[i + 1, j + 1])[0]
            below = below + EPSILON
            step = (up[0] / below, up[1] / below)
            moved = [times(step, p) for p in poly]
            for i in range(k + 1):
                coef[i] = (coef[i][0] + moved[i][0], coef[i][1] + moved[i][1])
            grown = poly + [(none, none)]
            for i in range(k + 1):
                grown[i + 1] = (grown[i + 1][0] - moved[i][0], grown[i + 1][1] - moved[i][1])
            poly = grown

        return [(jnp.broadcast_to(a, (16, lanes)), jnp.broadcast_to(b, (16, lanes))) for a, b in coef]

    def combine(wide, out_ref, keep_parts):
        def step(i, carry):
            x, y = i // chunks, pl.multiple_of(i % chunks * 16, 16)
            at = pl.ds(y, 16)
            mr, mi = real_ref[x + first, at, :], imag_ref[x + first, at, :]
            for comp in range(3):
                sr = jnp.zeros((16, lanes), F32)
                si = jnp.zeros((16, lanes), F32)
                for k in range(SWEEPS):
                    br, bi = basis[k, 0, comp, x + first, at, :], basis[k, 1, comp, x + first, at, :]
                    sr = sr + (wide[k][0] * br - wide[k][1] * bi)
                    si = si + (wide[k][0] * bi + wide[k][1] * br)
                for c, value in enumerate((mr * sr + mi * si, mr * si - mi * sr)):
                    out_ref[c, comp, x, at, :] = value
                    if keep_parts:
                        here = pl.ds(pl.multiple_of((comp * planes + x) * rows + y, 16), 16)
                        hi, lo = split(value)
                        field_hi[here, c * lanes : (c + 1) * lanes] = hi
                        field_lo[here, c * lanes : (c + 1) * lanes] = lo
            return carry

        lax.fori_loop(0, planes * chunks, step, 0, unroll=2)

    packs = [
        pltpu.make_async_remote_copy(
            src_ref=pack_ref, dst_ref=pack_in.at[me], send_sem=pack_s.at[d], recv_sem=pack_r.at[d],
            device_id={"slab": lax.rem(me + d, n)}, device_id_type=MESH,
        )
        for d in range(1, n)
    ]

    cap_row = lax.broadcasted_iota(jnp.int32, (CAP, lanes), 0).astype(F32)
    lane_sq = lax.broadcasted_iota(jnp.int32, (lanes, lanes), 1).astype(F32)
    row_sq = lax.broadcasted_iota(jnp.int32, (lanes, lanes), 0).astype(F32)
    earlier = jnp.where(row_sq < lane_sq, 1.0, 0.0).astype(F32)
    self_id = me.astype(F32)

    def compact(p, carry):
        pack = pack_in[p]
        owner, number, spot = pack[0:1, :], pack[1:2, :], pack[2:3, :]
        third = jnp.where(number >= 2.0 * planes * rows, 2.0, jnp.where(number >= 1.0 * planes * rows, 1.0, 0.0))
        inside = number - third * float(planes * rows)
        upper = inside - float((planes - WIDTH) * rows)
        low_place = jnp.where(upper >= 0.0, third * float(side_rows) + upper, -1.0)
        high_place = jnp.where(inside < float(side_rows), third * float(side_rows) + inside, -1.0)
        owned = [jnp.where(owner == self_id + shift, 1.0, 0.0) for shift in (0.0, -1.0, 1.0)]
        owned = jnp.concatenate(owned + [jnp.zeros((5, lanes), F32)], axis=0)
        rank = jnp.dot(owned, earlier, preferred_element_type=F32)
        at = pl.ds(pl.multiple_of(p * CAP, CAP), CAP)
        wanted = (
            (0, 0, number + 1.0), (1, 0, spot), (2, 0, pack[3:4, :]), (3, 0, pack[4:5, :]),
            (4, 1, low_place + 1.0), (5, 1, spot), (6, 2, high_place + 1.0), (7, 2, spot),
        )
        for k, target, value in wanted:
            hit = (cap_row == rank[target : target + 1, :]) & (owned[target : target + 1, :] > 0.0)
            found = jnp.sum(jnp.where(hit, value, 0.0), axis=1, keepdims=True)
            columns[k, at, :] = jnp.broadcast_to(found, (CAP, lanes))
        return carry

    def picks(p, carry):
        at = pl.ds(pl.multiple_of(p * CAP, CAP), CAP)
        place = columns[0, at, :] - 1.0
        for b in range(cells_rows // lanes):
            hot[at, b * lanes : (b + 1) * lanes] = jnp.where(
                lane_sq[:CAP] == place - float(b * lanes), 1.0, 0.0
            ).astype(BF16)
        return carry

    def placings(start, k, count):
        for q in range(slots // lanes):
            spot = columns[k, q * lanes : (q + 1) * lanes, :].T - 1.0

            def fill(b, carry):
                base = pl.multiple_of(b * lanes, lanes)
                hot_t[pl.ds(start + base, lanes), q * lanes : (q + 1) * lanes] = jnp.where(
                    row_sq + base.astype(F32) == spot, 1.0, 0.0
                ).astype(BF16)
                return carry

            lax.fori_loop(0, count // lanes, fill, 0)

    def spread_values(k, re, im):
        here = lane_of_slot == columns[k]
        for part_, value in enumerate((re, im)):
            hi, lo = split(jnp.where(here, value, 0.0))
            mis_hi[:, part_ * lanes : (part_ + 1) * lanes] = hi
            mis_lo[:, part_ * lanes : (part_ + 1) * lanes] = lo

    def add_source(start, x0, count, group):
        for comp in range(3):
            for x in range(0, count, group):
                begin_ = start + (comp * count + x) * rows
                block = hot_t[begin_ : begin_ + group * rows, :]
                added = jnp.dot(block, mis_hi[...], preferred_element_type=F32)
                added = added + jnp.dot(block, mis_lo[...], preferred_element_type=F32)
                for c in range(2):
                    basis[0, c, comp, x0 + x : x0 + x + group] = added[:, c * lanes : (c + 1) * lanes].reshape(
                        group, rows, lanes
                    )

    lane_of_slot = lax.broadcasted_iota(jnp.int32, (slots, lanes), 1).astype(F32)

    pl.semaphore_wait(barrier, n + nf - 2)
    send_down(0)
    send_up(0)
    loads[3].wait()
    loads[4].wait()
    loads[5].wait()
    edge = edge_ref[...]
    pack_ref[...] = jnp.concatenate(
        [
            owner_ref[...].astype(F32), (edge >> 7).astype(F32), (edge & 127).astype(F32), observed_ref[...],
            jnp.zeros((3, lanes), F32),
        ],
        axis=0,
    )
    for copy in packs:
        copy.start()
    pack_in[me] = pack_ref[...]
    lax.fori_loop(0, (planes - 2) * chunks, begin_inner, 0, unroll=4)

    def while_first():
        pair_sums(1)
        for copy in packs:
            copy.wait()
        lax.fori_loop(0, n, compact, 0)

    def while_second():
        pair_sums(2)
        lax.fori_loop(0, n, picks, 0)

    def while_third():
        pair_sums(3)
        placings(0, 0, cells_rows)
        placings(cells_rows, 4, 3 * side_rows)
        placings(cells_rows + 3 * side_rows, 6, 3 * side_rows)

    forward_sweep(0, lambda: None)
    forward_sweep(1, while_first)
    forward_sweep(2, while_second)
    forward_sweep(3, while_third)
    pair_sums(SWEEPS)
    for copy in gram_start(0):
        copy.wait()

    @pl.when(me > 0)
    def _():
        beside_copy(1).start()

    @pl.when(me < n - 1)
    def _():
        beside_copy(0).start()

    combine(coefficients(0), forward_ref, True)

    picked = jnp.dot(hot[...], field_hi[...], preferred_element_type=F32)
    picked = picked + jnp.dot(hot[...], field_lo[...], preferred_element_type=F32)
    here = lane_of_slot == columns[1]
    re = jnp.sum(jnp.where(here, picked[:, :lanes], 0.0), axis=1, keepdims=True) - columns[2]
    im = columns[3] - jnp.sum(jnp.where(here, picked[:, lanes:], 0.0), axis=1, keepdims=True)
    both = jnp.where(lane_of_slot == 0.0, re, jnp.where(lane_of_slot == 1.0, im, 0.0))
    mis_out[...] = both.T[0:8, :]

    @pl.when(me > 0)
    def _():
        misfit_copy(1).start()
        beside_copy(0).wait_recv()
        for copy in share_copies(0):
            copy.start()

    @pl.when(me < n - 1)
    def _():
        misfit_copy(0).start()
        beside_copy(1).wait_recv()
        for copy in share_copies(1):
            copy.start()

    spread_values(1, re, im)
    add_source(0, first, planes, 4)

    for side, there in enumerate((me > 0, me < n - 1)):
        start = 0 if side == 0 else last + 1

        @pl.when(there)
        def _(side=side, start=start):
            beside_copy(1 - side).wait_send()
            for copy in share_copies(side):
                copy.wait()
            for k in range(WIDTH):
                factors(start + k, inner, omega * beside[side, k * rows : (k + 1) * rows, :])
            misfit_copy(side).wait_recv()
            misfit_copy(1 - side).wait_send()

        @pl.when(jnp.logical_not(there))
        def _(side=side, start=start):
            mis_in[side] = jnp.zeros(mis_in.shape[1:], F32)
            for k in range(WIDTH):
                damp[start + k] = jnp.zeros((rows, lanes), F32)
                real_ref[start + k] = jnp.zeros((rows, lanes), F32)
                imag_ref[start + k] = jnp.zeros((rows, lanes), F32)

        column = jnp.concatenate([mis_in[side]] * (lanes // 8), axis=0).T
        spread_values(5 + 2 * side, column[:, 0:1], column[:, 1:2])
        add_source(cells_rows + side * 3 * side_rows, start, WIDTH, WIDTH)

    for t in range(SWEEPS):
        sweep(t, t, wide_planes - t - 1, True)
        if t:
            pair_sums(t)
    pair_sums(SWEEPS)
    for copy in gram_start(1):
        copy.wait()
    combine(coefficients(1), adjoint_ref, False)

    high_iota = lax.broadcasted_iota(jnp.int32, (high_blocks, lanes), 0)
    low_iota = lax.broadcasted_iota(jnp.int32, (LOW, lanes), 0)
    acc[...] = jnp.zeros(acc.shape, F32)

    def cells(i, carry):
        x, y = i // chunks, pl.multiple_of(i % chunks * 16, 16)
        value = jnp.zeros((16, lanes), F32)
        for comp in range(3):
            fr, fi = forward_ref[0, comp, x, pl.ds(y, 16), :], forward_ref[1, comp, x, pl.ds(y, 16), :]
            ar, ai = adjoint_ref[0, comp, x, pl.ds(y, 16), :], adjoint_ref[1, comp, x, pl.ds(y, 16), :]
            value = value + (ar * fi + ai * fr)
        value = omega * value
        ids = ids_ref[x, pl.ds(y, 16), :]
        high, low = ids >> 4, ids & (LOW - 1)
        hot = jnp.concatenate(
            [jnp.where(high[r : r + 1, :] == high_iota, 1.0, 0.0) for r in range(16)], axis=0
        ).astype(BF16)
        spot = jnp.concatenate(
            [jnp.where(low[r : r + 1, :] == low_iota, value[r : r + 1, :], 0.0) for r in range(16)], axis=0
        )
        acc[...] += lax.dot_general(
            jnp.concatenate([hot, hot], axis=1), jnp.concatenate(split(spot), axis=1),
            (((1,), (1,)), ((), ())), preferred_element_type=F32,
        )
        return carry

    lax.fori_loop(0, planes * chunks, cells, 0, unroll=4)
    wide_lane = lax.broadcasted_iota(jnp.int32, (high_blocks, 16 * LOW), 1)
    diagonal = jnp.zeros((high_blocks, 16 * LOW), F32)
    for r in range(16):
        inside = (wide_lane >= r * LOW) & (wide_lane < (r + 1) * LOW)
        diagonal = diagonal + jnp.where(inside, acc[r * high_blocks : (r + 1) * high_blocks, :], 0.0)
    folded = diagonal[:, :lanes] + diagonal[:, lanes:]
    for shift in (64, 32, 16):
        folded = folded + pltpu.roll(folded, shift, 1)
    fold_lane = lax.broadcasted_iota(jnp.int32, (8, lanes), 1) // LOW
    fold_row = lax.broadcasted_iota(jnp.int32, (8, lanes), 0)
    own = jnp.concatenate(
        [
            jnp.sum(jnp.where(fold_lane == fold_row, folded[8 * k : 8 * k + 8, :], 0.0), axis=0, keepdims=True)
            for k in range(high_blocks // 8)
        ],
        axis=0,
    )
    grad_out[...] = own
    for copy in spread(grad_out, grad_in, grad_s, grad_r, "slab", n, me):
        copy.wait()
    partial = total_of(own, grad_in, n, me)
    grad_out2[...] = partial
    for copy in spread(grad_out2, grad_in2, grad2_s, grad2_r, "freq", nf, mine):
        copy.wait()
    gradient_ref[...] = total_of(partial, grad_in2, nf, mine)


def write_kernel(forward_ref, adjoint_ref, gradient_ref, forward_out, adjoint_out, gradient_out, sems):
    copies = [
        pltpu.make_async_copy(src, dst, sems.at[k])
        for k, (src, dst) in enumerate([
            (forward_ref, forward_out), (adjoint_ref, adjoint_out), (gradient_ref, gradient_out),
        ])
    ]
    for copy in copies:
        copy.start()
    for copy in copies:
        copy.wait()


def body(source, omega, sigma_blocks, block_ids, rec_owner, rec_edge, observed):
    n, nf = lax.axis_size("slab"), lax.axis_size("freq")
    planes, rows, lanes = block_ids.shape
    blocks = sigma_blocks.shape[0]
    high_blocks = blocks // LOW
    vmem = pl.BlockSpec(memory_space=pltpu.VMEM)
    smem = pl.BlockSpec(memory_space=pltpu.SMEM)
    anywhere = pl.BlockSpec(memory_space=pl.ANY)
    cells_rows = 3 * planes * rows
    wide_planes = planes + 2 * WIDTH
    slots = n * CAP
    field = (2, 3, planes, rows, lanes)
    halo = pltpu.VMEM((SWEEPS, 2, 2, rows, lanes), F32)
    dma = pltpu.SemaphoreType.DMA
    grad_shape = (high_blocks // 8, lanes)
    grad = pltpu.VMEM(grad_shape, F32)
    wide = pltpu.VMEM((wide_planes, rows, lanes), F32)
    operands = (
        source[0], sigma_blocks.reshape(-1, lanes), block_ids, rec_owner.reshape(1, -1), rec_edge.reshape(1, -1),
        observed[0],
    )
    operands = [pltpu.with_memory_space_constraint(a, pltpu.HBM) for a in operands]
    results = pl.pallas_call(
        functools.partial(kernel, n, nf, high_blocks),
        out_shape=(pltpu.VMEM(field, F32), pltpu.VMEM(field, F32), pltpu.VMEM(grad_shape, F32)),
        in_specs=[smem] + [anywhere] * 6,
        out_specs=(vmem, vmem, vmem),
        scratch_shapes=[
            pltpu.VMEM(field, BF16),
            pltpu.VMEM((blocks // lanes, lanes), F32),
            pltpu.VMEM((planes, rows, lanes), jnp.int32),
            pltpu.VMEM((1, lanes), jnp.int32),
            pltpu.VMEM((1, lanes), jnp.int32),
            pltpu.VMEM((2, lanes), F32),
            wide, wide, wide,
            pltpu.VMEM((planes * rows, lanes), F32),
            pltpu.VMEM((2, WIDTH * rows, lanes), F32),
            pltpu.VMEM((8, lanes), F32),
            pltpu.VMEM((8, slots), F32),
            pltpu.VMEM((2, 8, slots), F32),
            pltpu.VMEM((SWEEPS + 1, 2, 3, wide_planes, rows, lanes), F32),
            pltpu.VMEM((2, 3, wide_planes, rows + 8, lanes), F32),
            pltpu.VMEM((2, 3, wide_planes, rows + 8, lanes), F32),
            halo, halo, halo, halo,
            pltpu.VMEM((COUNT, lanes), F32),
            pltpu.VMEM((2, 1, lanes), F32),
            pltpu.VMEM((2, n, 1, lanes), F32),
            pltpu.VMEM((n, 8, lanes), F32),
            grad,
            pltpu.VMEM((n,) + grad_shape, F32),
            grad,
            pltpu.VMEM((nf,) + grad_shape, F32),
            pltpu.VMEM((8, slots, lanes), F32),
            pltpu.VMEM((slots, cells_rows), BF16),
            pltpu.VMEM((3 * wide_planes * rows, slots), BF16),
            pltpu.VMEM((cells_rows, 2 * lanes), BF16),
            pltpu.VMEM((cells_rows, 2 * lanes), BF16),
            pltpu.VMEM((slots, 2 * lanes), BF16),
            pltpu.VMEM((slots, 2 * lanes), BF16),
            pltpu.VMEM((16 * high_blocks, 16 * LOW), F32),
            dma((6,)),
            dma((SWEEPS,)), dma((SWEEPS,)), dma((SWEEPS,)), dma((SWEEPS,)),
            dma((2, n)), dma((2, n)),
            dma((n,)), dma((n,)),
            dma((n,)), dma((n,)),
            dma((nf,)), dma((nf,)),
            dma((4,)), dma((4,)),
            dma((2, nf)), dma((2, nf)),
        ],
        compiler_params=pltpu.CompilerParams(
            collective_id=0, has_side_effects=True, vmem_limit_bytes=50 * 1024 * 1024
        ),
        name="solves",
    )(omega, *operands)
    forward, adjoint, gradient = pl.pallas_call(
        write_kernel,
        out_shape=(
            jax.ShapeDtypeStruct(field, F32), jax.ShapeDtypeStruct(field, F32), jax.ShapeDtypeStruct(grad_shape, F32),
        ),
        in_specs=[anywhere] * 3,
        out_specs=(anywhere,) * 3,
        scratch_shapes=[dma((3,))],
        name="write",
    )(*results)
    return forward[None], adjoint[None], gradient.reshape(blocks)


def solution(mesh):
    return jax.shard_map(
        body,
        mesh=mesh,
        in_specs=(
            P("freq", None, None, "slab", None, None),
            P("freq"),
            P(),
            P("slab", None, None),
            P("slab", None),
            P("slab"),
            P("freq", None, "slab"),
        ),
        out_specs=(
            P("freq", None, None, "slab", None, None),
            P("freq", None, None, "slab", None, None),
            P(),
        ),
        check_vma=False,
    )
```

time: 104 us -> 177 us (1.70)
  Pallas kernels: 93 us -> 173 us
  local copies, waits for them, and re-layouts: 9.65 us -> 2.88 us
    pallas_call x1, Pallas kernels: 2.63 us -> 96.4 us  [body(): pl.pallas_call(write_kernel, out_shape=(jax.ShapeDtypeStruct(field, F32),...]
    pallas_call x1, Pallas kernels: 90.4 us -> 76.1 us  [body(): pl.pallas_call(functools.partial(kernel, n, nf, high_blocks), out_shape=(...]
    unnamed x16 -> x6, local copies, waits for them, and re-layouts: 9.01 us -> 2.88 us
where the time goes in v1:
time: 177 us
  Pallas kernels  173 us (98%)
  local copies, waits for them, and re-layouts  2.88 us (2%)
    pallas_call x1, Pallas kernels, body(): pl.pallas_call(write_kernel, out_shape=(jax.ShapeDtypeStruct(field, F32),...  96.4 us
    pallas_call x1, Pallas kernels, body(): pl.pallas_call(functools.partial(kernel, n, nf, high_blocks), out_shape=(...  76.1 us

profile of v1, /device:TPU:0, one launch (start us, length us, event | category | flops | bytes accessed | tf_op | source)
XLA Modules:
  0.0 176.8 jit_solution(1690143409434563570)
XLA Ops:
  1.3 76.1 %solves.1 = (f32[2,3,8,64,128]{4,3,2,1,0:T(8,128)S(1)}, f32[2,3,8,64,128]{4,3,2,1,0:T(8,128)S(1)}, f32[2,128]{1,0:T(2,128)S(1)}) custom-call(f32[1]{0:T(128)S(6)} %copy.10.omega_ref, bf16[2,3,8,64,128]{4,3,2,1,0:T(8,128)(2,1)} %bitcast.8, f32[2,128]{1,0:T(2,128)} %bitcast.9, s32[8,64,128]{2,1,0:T(8,128)} %ids_hbm.1, s32[1,128]{1,0:T(1,128)} %bitcast.11, ...), custom_call_target="tpu_custom_call" | custom-call | tf_op jit(solution)/shard_map/solves/pallas_call | solution.py:672
  77.4 0.0 copy-start
  77.4 1.2 copy-done
  78.6 0.0 copy-start.1
  78.6 1.1 copy-done.1
  79.7 0.0 copy-start.2
  79.7 0.6 copy-done.2
  80.3 96.4 %write.1 = (f32[2,3,8,64,128]{4,3,2,1,0:T(8,128)}, f32[2,3,8,64,128]{4,3,2,1,0:T(8,128)}, f32[2,128]{1,0:T(2,128)}) custom-call(f32[2,3,8,64,128]{4,3,2,1,0:T(8,128)} %copy-done, f32[2,3,8,64,128]{4,3,2,1,0:T(8,128)} %copy-done.1, f32[2,128]{1,0:T(2,128)} %copy-done.2), custom_call_target="tpu_custom_call" | custom-call | tf_op jit(solution)/shard_map/write/pallas_call | solution.py:724
Async XLA Ops:
  77.4 1.2 copy-start
  78.6 1.2 copy-start.1
  79.7 0.6 copy-start.2

commit v2 on v1

--- a/solution.py
+++ b/solution.py
@@ -726,11 +726,11 @@
         out_shape=(
             jax.ShapeDtypeStruct(field, F32), jax.ShapeDtypeStruct(field, F32), jax.ShapeDtypeStruct(grad_shape, F32),
         ),
-        in_specs=[anywhere] * 3,
+        in_specs=[vmem] * 3,
         out_specs=(anywhere,) * 3,
         scratch_shapes=[dma((3,))],
         name="write",
-    )(*results)
+    )(*[pltpu.with_memory_space_constraint(a, pltpu.VMEM) for a in results])
     return forward[None], adjoint[None], gradient.reshape(blocks)
 
 

time: 177 us -> 79.3 us (0.45)
  Pallas kernels: 173 us -> 77.8 us
  local copies, waits for them, and re-layouts: 2.88 us -> 0 us
    pallas_call x1, Pallas kernels: 96.4 us -> 1.69 us  [body(): pl.pallas_call(write_kernel, out_shape=(jax.ShapeDtypeStruct(field, F32),...]
    unnamed x6 -> x0, local copies, waits for them, and re-layouts: 2.88 us -> none
where the time goes in v2:
time: 79.3 us; the launch traced here: 79.1 us
  Pallas kernels  77.8 us (98%)
  between operations  1.29 us (2%)
    pallas_call x1, Pallas kernels, body(): pl.pallas_call(functools.partial(kernel, n, nf, high_blocks), out_shape=(...  76.1 us
    pallas_call x1, Pallas kernels, body(): pl.pallas_call(write_kernel, out_shape=(jax.ShapeDtypeStruct(field, F32),...  1.69 us

profile of v2, /device:TPU:0, one launch (start us, length us, event | category | flops | bytes accessed | tf_op | source)
XLA Modules:
  0.0 79.1 jit_solution(14369205845364412329)
XLA Ops:
  1.3 76.1 %solves.1 = (f32[2,3,8,64,128]{4,3,2,1,0:T(8,128)S(1)}, f32[2,3,8,64,128]{4,3,2,1,0:T(8,128)S(1)}, f32[2,128]{1,0:T(2,128)S(1)}) custom-call(f32[1]{0:T(128)S(6)} %copy.10.omega_ref, bf16[2,3,8,64,128]{4,3,2,1,0:T(8,128)(2,1)} %bitcast.8, f32[2,128]{1,0:T(2,128)} %bitcast.9, s32[8,64,128]{2,1,0:T(8,128)} %ids_hbm.1, s32[1,128]{1,0:T(1,128)} %bitcast.11, ...), custom_call_target="tpu_custom_call" | custom-call | tf_op jit(solution)/shard_map/solves/pallas_call | solution.py:672
  77.4 1.7 %write.1 = (f32[2,3,8,64,128]{4,3,2,1,0:T(8,128)}, f32[2,3,8,64,128]{4,3,2,1,0:T(8,128)}, f32[2,128]{1,0:T(2,128)}) custom-call(f32[2,3,8,64,128]{4,3,2,1,0:T(8,128)S(1)} %get-tuple-element.9.forward_ref, f32[2,3,8,64,128]{4,3,2,1,0:T(8,128)S(1)} %get-tuple-element.10.adjoint_ref, f32[2,128]{1,0:T(2,128)S(1)} %get-tuple-element.11.gradient_ref), custom_call_target="tpu_custom_call" | custom-call | tf_op jit(solution)/shard_map/write/pallas_call | solution.py:724

commit v3 on v2

--- a/solution.py
+++ b/solution.py
@@ -31,9 +31,9 @@
     source_ref, sigma_ref, ids_ref, owner_ref, edge_ref, observed_ref,
     damp, real_ref, imag_ref, cond, beside, pack_ref, mis_out, mis_in,
     basis, zb, curl, up_out, down_out, low_in, high_in,
-    gram_acc, gram_out, gram_in, pack_in, grad_out, grad_in, grad_out2, grad_in2,
+    gram_acc, gram_out, gram_in, pack_in, grad_out, grad_in,
     columns, hot, hot_t, field_hi, field_lo, mis_hi, mis_lo, acc,
-    local_s, up_s, up_r, down_s, down_r, gram_s, gram_r, pack_s, pack_r, grad_s, grad_r, grad2_s, grad2_r,
+    local_s, up_s, up_r, down_s, down_r, gram_s, gram_r, pack_s, pack_r, grad_s, grad_r,
     near_s, near_r, share_s, share_r,
 ):
     me = lax.axis_index("slab")
@@ -57,10 +57,11 @@
         copy.start()
 
     barrier = pltpu.get_barrier_semaphore()
-    for d in range(1, n):
-        pl.semaphore_signal(barrier, inc=1, device_id={"slab": lax.rem(me + d, n)}, device_id_type=MESH)
-    for d in range(1, nf):
-        pl.semaphore_signal(barrier, inc=1, device_id={"freq": lax.rem(mine + d, nf)}, device_id_type=MESH)
+    for k in range(1, n * nf):
+        pl.semaphore_signal(
+            barrier, inc=1, device_id={"slab": lax.rem(me + k // nf, n), "freq": lax.rem(mine + k % nf, nf)},
+            device_id_type=MESH,
+        )
 
     def spread(src, dst, send, recv, axis, count, position):
         copies = []
@@ -81,17 +82,16 @@
         return total
 
     lane = lax.broadcasted_iota(jnp.int32, (rows, lanes), 1)
-    row = lax.broadcasted_iota(jnp.int32, (rows, lanes), 0)
     inner = slice(0, rows)
     above = slice(1, rows + 1)
     shifted = slice(8, rows + 8)
     under = slice(7, rows + 7)
 
     def f3(v):
-        return jnp.where(lane == lanes - 1, 0.0, pltpu.roll(v, lanes - 1, 1)) - v
+        return jnp.where(lane[: v.shape[0]] == lanes - 1, 0.0, pltpu.roll(v, lanes - 1, 1)) - v
 
     def g3(v):
-        return jnp.where(lane == 0, 0.0, pltpu.roll(v, 1, 1)) - v
+        return jnp.where(lane[: v.shape[0]] == 0, 0.0, pltpu.roll(v, 1, 1)) - v
 
     valid = jnp.where(me > 0, 1.0, 0.0).astype(F32)
     omega = omega_ref[0]
@@ -167,35 +167,48 @@
             recv_sem=near_r.at[2 + side], device_id={"slab": lax.rem(to, n)}, device_id_type=MESH,
         )
 
-    def up_copy(slot):
+    def cut_of(t):
+        return rows // 8 // 2 * 8 + 8 * (1 - t)
+
+    def rows_of(t, half):
+        return (0, cut_of(t)) if half == 0 else (cut_of(t), rows)
+
+    def span(t, half):
+        lo, hi = rows_of(t, half)
+        return pl.ds(4 * lo, 4 * (hi - lo))
+
+    def place_of(t, half, c, k):
+        lo, hi = rows_of(t, half)
+        start = 4 * lo + (2 * c + k) * (hi - lo)
+        return slice(start, start + hi - lo)
+
+    def up_copy(t, half):
+        at = span(t, half)
         return pltpu.make_async_remote_copy(
-            src_ref=up_out.at[slot], dst_ref=low_in.at[slot], send_sem=up_s.at[slot],
-            recv_sem=up_r.at[slot], device_id={"slab": lax.rem(me + 1, n)}, device_id_type=MESH,
-        )
-
-    def down_copy(slot):
+            src_ref=up_out.at[t, at], dst_ref=low_in.at[t, at], send_sem=up_s.at[t, half],
+            recv_sem=up_r.at[t, half], device_id={"slab": lax.rem(me + 1, n)}, device_id_type=MESH,
+        )
+
+    def down_copy(t, half):
+        at = span(t, half)
         return pltpu.make_async_remote_copy(
-            src_ref=down_out.at[slot], dst_ref=high_in.at[slot], send_sem=down_s.at[slot],
-            recv_sem=down_r.at[slot], device_id={"slab": lax.rem(me + n - 1, n)}, device_id_type=MESH,
-        )
-
-    def precondition(t, x):
-        mr, mi = real_ref[x], imag_ref[x]
+            src_ref=down_out.at[t, at], dst_ref=high_in.at[t, at], send_sem=down_s.at[t, half],
+            recv_sem=down_r.at[t, half], device_id={"slab": lax.rem(me + n - 1, n)}, device_id_type=MESH,
+        )
+
+    def precondition(t, x, at=inner):
+        mr, mi = real_ref[x, at], imag_ref[x, at]
         for comp in range(3):
-            br, bi = basis[t, 0, comp, x], basis[t, 1, comp, x]
-            zb[0, comp, x, inner] = mr * br + mi * bi
-            zb[1, comp, x, inner] = mr * bi - mi * br
-
-    def curls(x, ahead=None):
+            br, bi = basis[t, 0, comp, x, at], basis[t, 1, comp, x, at]
+            zb[0, comp, x, at] = mr * br + mi * bi
+            zb[1, comp, x, at] = mr * bi - mi * br
+
+    def curls(x):
         for c in range(2):
             e1, e2, e3 = zb[c, 0, x, inner], zb[c, 1, x, inner], zb[c, 2, x, inner]
-            if ahead is None:
-                e2n, e3n = zb[c, 1, x + 1, inner], zb[c, 2, x + 1, inner]
-            else:
-                e2n, e3n = ahead[c, 0], ahead[c, 1]
             curl[c, 0, x, shifted] = (zb[c, 2, x, above] - e3) - f3(e2)
-            curl[c, 1, x, shifted] = f3(e1) - (e3n - e3)
-            curl[c, 2, x, shifted] = (e2n - e2) - (zb[c, 0, x, above] - e1)
+            curl[c, 1, x, shifted] = f3(e1) - (zb[c, 2, x + 1, inner] - e3)
+            curl[c, 2, x, shifted] = (zb[c, 1, x + 1, inner] - e2) - (zb[c, 0, x, above] - e1)
 
     def images(t, x, keep=None):
         damping = damp[x]
@@ -213,105 +226,175 @@
                 turned = damping * zb[1 - c, comp, x, inner]
                 basis[t + 1, c, comp, x] = parts[comp] - turned if c == 0 else parts[comp] + turned
 
-    def sweep(t, lo, hi, masked):
+    def sweep_inner(t):
+        for k in range(1, 4):
+            precondition(t, first + k)
+        curls(first)
+        curls(first + 1)
+
+        def step(x, carry):
+            images(t, x)
+            curls(x + 1)
+            precondition(t, x + 3)
+            return carry
+
+        lax.fori_loop(first + 1, last - 3, step, 0)
+        images(t, last - 3)
+        curls(last - 2)
+        images(t, last - 2)
+        curls(last - 1)
+        images(t, last - 1)
+        for c in range(2):
+            def turn(x, comp):
+                turned = damp[x] * zb[1 - c, comp, x, inner]
+                return turned if c else -turned
+
+            b1, b2, b3 = (curl[c, k, first, shifted] for k in range(3))
+            basis[t + 1, c, 0, first] = g3(b2) - (curl[c, 2, first, under] - b3) + turn(first, 0)
+            basis[t + 1, c, 1, first] = turn(first, 1) - b3 - g3(b1)
+            basis[t + 1, c, 2, first] = (curl[c, 0, first, under] - b1) + b2 + turn(first, 2)
+            e2, e3 = zb[c, 1, last, inner], zb[c, 2, last, inner]
+            b1 = (zb[c, 2, last, above] - e3) - f3(e2)
+            curl[c, 0, last, shifted] = b1
+            basis[t + 1, c, 0, last] = turn(last, 0)
+            basis[t + 1, c, 1, last] = turn(last, 1) + curl[c, 2, last - 1, shifted] - g3(b1)
+            basis[t + 1, c, 2, last] = turn(last, 2) - curl[c, 1, last - 1, shifted]
+            basis[t + 1, c, 2, last] += curl[c, 0, last, under] - b1
+
+    def send_down(t, half):
+        lo, hi = rows_of(t, half)
+        for c in range(2):
+            for k in range(2):
+                down_out[t, place_of(t, half, c, k)] = zb[c, 1 + k, first, lo:hi]
+
+        @pl.when(me > 0)
+        def _():
+            down_copy(t, half).start()
+
+    def send_up(t, half):
+        lo, hi = rows_of(t, half)
+        for c in range(2):
+            e1 = zb[c, 0, last, lo:hi]
+            up_out[t, place_of(t, half, c, 0)] = f3(e1) + zb[c, 2, last, lo:hi]
+            up_out[t, place_of(t, half, c, 1)] = (zb[c, 0, last, lo + 1 : hi + 1] - e1) + zb[c, 1, last, lo:hi]
+
+        @pl.when(me < n - 1)
+        def _():
+            up_copy(t, half).start()
+
+    def receive(t, half):
+        lo, hi = rows_of(t, half)
+        at = slice(lo, hi)
+
+        @pl.when(me > 0)
+        def _():
+            up_copy(t, half).wait_recv()
+
+        for c in range(2):
+            b2p = (low_in[t, place_of(t, half, c, 0)] - zb[c, 2, first, at]) * valid
+            b3p = (zb[c, 1, first, at] - low_in[t, place_of(t, half, c, 1)]) * valid
+            basis[t + 1, c, 1, first, at] += b3p
+            basis[t + 1, c, 2, first, at] -= b2p
+        if t < SWEEPS - 1:
+            precondition(t + 1, first, at)
+            send_down(t + 1, half)
+
+        @pl.when(me < n - 1)
+        def _():
+            down_copy(t, half).wait_recv()
+
+        for c in range(2):
+            b2 = up_out[t, place_of(t, half, c, 0)] - high_in[t, place_of(t, half, c, 1)]
+            b3 = high_in[t, place_of(t, half, c, 0)] - up_out[t, place_of(t, half, c, 1)]
+            curl[c, 2, last, lo + 8 : hi + 8] = b3
+            basis[t + 1, c, 0, last, at] += g3(b2) - (curl[c, 2, last, lo + 7 : hi + 7] - b3)
+            basis[t + 1, c, 1, last, at] -= b3
+            basis[t + 1, c, 2, last, at] += b2
+        if t < SWEEPS - 1:
+            precondition(t + 1, last, at)
+            send_up(t + 1, half)
+
+    def forward_sweep(t, before, between):
+        sweep_inner(t)
+        before()
+        receive(t, 0)
+        between()
+        receive(t, 1)
+
+    def forward_sent():
+        for t in range(SWEEPS):
+            for half in range(2):
+                @pl.when(me > 0)
+                def _(t=t, half=half):
+                    down_copy(t, half).wait_send()
+
+                @pl.when(me < n - 1)
+                def _(t=t, half=half):
+                    up_copy(t, half).wait_send()
+
+    per = rows // 8
+
+    def products(j_, x, at, sums):
+        sums = list(sums)
+        for comp in range(3):
+            re = [basis[k, 0, comp, x, at, :] for k in range(j_ + 1)]
+            im = [basis[k, 1, comp, x, at, :] for k in range(j_ + 1)]
+            for i_ in range(j_ + 1):
+                sums[2 * i_] = sums[2 * i_] + (re[i_] * re[j_] + im[i_] * im[j_])
+                if i_ != j_:
+                    sums[2 * i_ + 1] = sums[2 * i_ + 1] + (re[i_] * im[j_] - im[i_] * re[j_])
+        return tuple(sums)
+
+    def blank_sums(j_):
+        return (jnp.zeros((8, lanes), F32),) * (2 * j_ + 1)
+
+    def keep_sums(j_, sums):
+        for k in range(2 * j_ + 1):
+            at = j_ * j_ - 1 + k
+            gram_acc[at : at + 1, :] = jnp.sum(sums[k], axis=0, keepdims=True)
+
+    def pair_sums(j_, start, step, count, sums):
+        def body_(i, sums):
+            return products(j_, i // per * step + start, pl.ds(pl.multiple_of(i % per * 8, 8), 8), sums)
+
+        return lax.fori_loop(0, count * per, body_, sums, unroll=2)
+
+    def all_sums(j_):
+        keep_sums(j_, pair_sums(j_, first, 1, planes, blank_sums(j_)))
+
+    def sweep(t):
+        lo, hi = t, wide_planes - t - 1
+        wanted = [t] if 0 < t < SWEEPS - 1 else [t, t + 1] if t else []
         for k in range(4):
             precondition(t, lo + k)
         curls(lo)
         curls(lo + 1)
 
-        def keep_of(x):
-            if not masked:
-                return None
-            return jnp.where((x == first) & (me == 0), 0.0, 1.0).astype(F32)
-
-        def step(x, carry):
-            images(t, x, keep_of(x))
+        def gather(x, sums):
+            return tuple(
+                functools.reduce(lambda held, y: products(j, x, slice(y, y + 8), held), range(0, rows, 8), own)
+                for j, own in zip(wanted, sums)
+            )
+
+        def step(x, carry, inside):
+            keep = jnp.where((x == first) & (me == 0), 0.0, 1.0).astype(F32) if inside else None
+            images(t, x, keep)
             curls(x + 1)
             precondition(t, x + 3)
-            return carry
-
-        lax.fori_loop(lo + 1, hi - 2, step, 0)
+            return gather(x, carry) if inside else carry
+
+        sums = tuple(blank_sums(j) for j in wanted)
+        top = min(hi - 2, last + 1)
+        lax.fori_loop(lo + 1, first, lambda x, carry: step(x, carry, False), 0)
+        sums = lax.fori_loop(first, top, lambda x, carry: step(x, carry, True), sums)
+        lax.fori_loop(top, hi - 2, lambda x, carry: step(x, carry, False), 0)
         images(t, hi - 2)
         curls(hi - 1)
         images(t, hi - 1)
-
-    def send_down(t):
-        precondition(t, first)
-        for c in range(2):
-            down_out[t, c, 0] = zb[c, 1, first, inner]
-            down_out[t, c, 1] = zb[c, 2, first, inner]
-
-        @pl.when(me > 0)
-        def _():
-            down_copy(t).start()
-
-    def send_up(t):
-        precondition(t, last)
-        for c in range(2):
-            e1 = zb[c, 0, last, inner]
-            up_out[t, c, 0] = f3(e1) + zb[c, 2, last, inner]
-            up_out[t, c, 1] = (zb[c, 0, last, above] - e1) + zb[c, 1, last, inner]
-
-        @pl.when(me < n - 1)
-        def _():
-            up_copy(t).start()
-
-    def forward_sweep(t, meanwhile):
-        sweep(t, first, last, False)
-        meanwhile()
-
-        @pl.when(me > 0)
-        def _():
-            up_copy(t).wait_recv()
-            down_copy(t).wait_send()
-
-        @pl.when(me == 0)
-        def _():
-            low_in[t] = jnp.zeros(low_in.shape[1:], F32)
-
-        for c in range(2):
-            curl[c, 1, first - 1, shifted] = (low_in[t, c, 0] - zb[c, 2, first, inner]) * valid
-            curl[c, 2, first - 1, shifted] = (zb[c, 1, first, inner] - low_in[t, c, 1]) * valid
-        images(t, first)
-        if t < SWEEPS - 1:
-            send_down(t + 1)
-
-        @pl.when(me < n - 1)
-        def _():
-            down_copy(t).wait_recv()
-            up_copy(t).wait_send()
-
-        @pl.when(me == n - 1)
-        def _():
-            high_in[t] = jnp.zeros(high_in.shape[1:], F32)
-
-        curls(last, high_in.at[t])
-        images(t, last)
-        if t < SWEEPS - 1:
-            send_up(t + 1)
-
-    per = rows // 8
-
-    def pair_sums(j_):
-        width = 2 * j_ + 1
-
-        def products(i, sums):
-            x, y = i // per + first, pl.multiple_of(i % per * 8, 8)
-            sums = list(sums)
-            for comp in range(3):
-                re = [basis[k, 0, comp, x, pl.ds(y, 8), :] for k in range(j_ + 1)]
-                im = [basis[k, 1, comp, x, pl.ds(y, 8), :] for k in range(j_ + 1)]
-                for i_ in range(j_ + 1):
-                    sums[2 * i_] = sums[2 * i_] + (re[i_] * re[j_] + im[i_] * im[j_])
-                    if i_ != j_:
-                        sums[2 * i_ + 1] = sums[2 * i_ + 1] + (re[i_] * im[j_] - im[i_] * re[j_])
-            return tuple(sums)
-
-        zero = jnp.zeros((8, lanes), F32)
-        sums = lax.fori_loop(0, planes * per, products, (zero,) * width, unroll=2)
-        for k in range(width):
-            at = j_ * j_ - 1 + k
-            gram_acc[at : at + 1, :] = jnp.sum(sums[k], axis=0, keepdims=True)
+        for x in range(top, last + 1):
+            sums = gather(x, sums)
+        for j, own in zip(wanted, sums):
+            keep_sums(j, own)
 
     gram_lane = lax.broadcasted_iota(jnp.int32, (COUNT, lanes), 1)
     gram_row = lax.broadcasted_iota(jnp.int32, (COUNT, lanes), 0)
@@ -468,9 +551,21 @@
 
     lane_of_slot = lax.broadcasted_iota(jnp.int32, (slots, lanes), 1).astype(F32)
 
-    pl.semaphore_wait(barrier, n + nf - 2)
-    send_down(0)
-    send_up(0)
+    precondition(0, first)
+    precondition(0, last)
+
+    @pl.when(me == 0)
+    def _():
+        low_in[...] = jnp.zeros(low_in.shape, F32)
+
+    @pl.when(me == n - 1)
+    def _():
+        high_in[...] = jnp.zeros(high_in.shape, F32)
+
+    pl.semaphore_wait(barrier, n * nf - 1)
+    for half in range(2):
+        send_down(0, half)
+        send_up(0, half)
     loads[3].wait()
     loads[4].wait()
     loads[5].wait()
@@ -487,28 +582,33 @@
     pack_in[me] = pack_ref[...]
     lax.fori_loop(0, (planes - 2) * chunks, begin_inner, 0, unroll=4)
 
-    def while_first():
-        pair_sums(1)
+    def nothing():
+        pass
+
+    def receive_packs():
+        all_sums(2)
         for copy in packs:
             copy.wait()
         lax.fori_loop(0, n, compact, 0)
 
-    def while_second():
-        pair_sums(2)
-        lax.fori_loop(0, n, picks, 0)
-
-    def while_third():
-        pair_sums(3)
-        placings(0, 0, cells_rows)
-        placings(cells_rows, 4, 3 * side_rows)
-        placings(cells_rows + 3 * side_rows, 6, 3 * side_rows)
-
-    forward_sweep(0, lambda: None)
-    forward_sweep(1, while_first)
-    forward_sweep(2, while_second)
-    forward_sweep(3, while_third)
-    pair_sums(SWEEPS)
-    for copy in gram_start(0):
+    last_sums = []
+
+    def near_last():
+        all_sums(3)
+        last_sums.append(pair_sums(SWEEPS, first + 1, 1, planes - 2, blank_sums(SWEEPS)))
+
+    forward_sweep(0, nothing, nothing)
+    forward_sweep(1, nothing, functools.partial(all_sums, 1))
+    forward_sweep(2, nothing, receive_packs)
+    forward_sweep(3, nothing, near_last)
+    keep_sums(SWEEPS, pair_sums(SWEEPS, first, planes - 1, 2, last_sums[0]))
+    sums_sent = gram_start(0)
+    forward_sent()
+    lax.fori_loop(0, n, picks, 0)
+    placings(0, 0, cells_rows)
+    placings(cells_rows, 4, 3 * side_rows)
+    placings(cells_rows + 3 * side_rows, 6, 3 * side_rows)
+    for copy in sums_sent:
         copy.wait()
 
     @pl.when(me > 0)
@@ -572,10 +672,7 @@
         add_source(cells_rows + side * 3 * side_rows, start, WIDTH, WIDTH)
 
     for t in range(SWEEPS):
-        sweep(t, t, wide_planes - t - 1, True)
-        if t:
-            pair_sums(t)
-    pair_sums(SWEEPS)
+        sweep(t)
     for copy in gram_start(1):
         copy.wait()
     combine(coefficients(1), adjoint_ref, False)
@@ -625,13 +722,23 @@
         axis=0,
     )
     grad_out[...] = own
-    for copy in spread(grad_out, grad_in, grad_s, grad_r, "slab", n, me):
+    copies = []
+    for k in range(1, n * nf):
+        copy = pltpu.make_async_remote_copy(
+            src_ref=grad_out, dst_ref=grad_in.at[k], send_sem=grad_s.at[k], recv_sem=grad_r.at[k],
+            device_id={"slab": lax.rem(me + k // nf, n), "freq": lax.rem(mine + k % nf, nf)}, device_id_type=MESH,
+        )
+        copy.start()
+        copies.append(copy)
+    grad_in[0] = own
+    for copy in copies:
         copy.wait()
-    partial = total_of(own, grad_in, n, me)
-    grad_out2[...] = partial
-    for copy in spread(grad_out2, grad_in2, grad2_s, grad2_r, "freq", nf, mine):
-        copy.wait()
-    gradient_ref[...] = total_of(partial, grad_in2, nf, mine)
+
+    def add_one(k, total):
+        a, f = k // nf, k % nf
+        return total + grad_in[lax.rem(me - a + n, n) * nf + lax.rem(mine - f + nf, nf)]
+
+    gradient_ref[...] = lax.fori_loop(0, n * nf, add_one, jnp.zeros(own.shape, F32), unroll=4)
 
 
 def write_kernel(forward_ref, adjoint_ref, gradient_ref, forward_out, adjoint_out, gradient_out, sems):
@@ -659,7 +766,7 @@
     wide_planes = planes + 2 * WIDTH
     slots = n * CAP
     field = (2, 3, planes, rows, lanes)
-    halo = pltpu.VMEM((SWEEPS, 2, 2, rows, lanes), F32)
+    halo = pltpu.VMEM((SWEEPS, 4 * rows, lanes), F32)
     dma = pltpu.SemaphoreType.DMA
     grad_shape = (high_blocks // 8, lanes)
     grad = pltpu.VMEM(grad_shape, F32)
@@ -696,9 +803,7 @@
             pltpu.VMEM((2, n, 1, lanes), F32),
             pltpu.VMEM((n, 8, lanes), F32),
             grad,
-            pltpu.VMEM((n,) + grad_shape, F32),
-            grad,
-            pltpu.VMEM((nf,) + grad_shape, F32),
+            pltpu.VMEM((n * nf,) + grad_shape, F32),
             pltpu.VMEM((8, slots, lanes), F32),
             pltpu.VMEM((slots, cells_rows), BF16),
             pltpu.VMEM((3 * wide_planes * rows, slots), BF16),
@@ -708,11 +813,10 @@
             pltpu.VMEM((slots, 2 * lanes), BF16),
             pltpu.VMEM((16 * high_blocks, 16 * LOW), F32),
             dma((6,)),
-            dma((SWEEPS,)), dma((SWEEPS,)), dma((SWEEPS,)), dma((SWEEPS,)),
+            dma((SWEEPS, 2)), dma((SWEEPS, 2)), dma((SWEEPS, 2)), dma((SWEEPS, 2)),
             dma((2, n)), dma((2, n)),
             dma((n,)), dma((n,)),
-            dma((n,)), dma((n,)),
-            dma((nf,)), dma((nf,)),
+            dma((n * nf,)), dma((n * nf,)),
             dma((4,)), dma((4,)),
             dma((2, nf)), dma((2, nf)),
         ],

time: 79.3 us -> 74.8 us (0.943)
  Pallas kernels: 77.8 us -> 73.3 us
    pallas_call x1, Pallas kernels: 76.1 us -> 71.6 us  [body(): pl.pallas_call(functools.partial(kernel, n, nf, high_blocks), out_shape=(...]
where the time goes in v3:
time: 74.8 us; the launch traced here: 74.6 us
  Pallas kernels  73.3 us (98%)
  between operations  1.29 us (2%)
    pallas_call x1, Pallas kernels, body(): pl.pallas_call(functools.partial(kernel, n, nf, high_blocks), out_shape=(...  71.6 us
    pallas_call x1, Pallas kernels, body(): pl.pallas_call(write_kernel, out_shape=(jax.ShapeDtypeStruct(field, F32),...  1.69 us

profile of v3, /device:TPU:0, one launch (start us, length us, event | category | flops | bytes accessed | tf_op | source)
XLA Modules:
  0.0 74.6 jit_solution(3112939194911896058)
XLA Ops:
  1.3 71.6 %solves.1 = (f32[2,3,8,64,128]{4,3,2,1,0:T(8,128)S(1)}, f32[2,3,8,64,128]{4,3,2,1,0:T(8,128)S(1)}, f32[2,128]{1,0:T(2,128)S(1)}) custom-call(f32[1]{0:T(128)S(6)} %copy.10.omega_ref, bf16[2,3,8,64,128]{4,3,2,1,0:T(8,128)(2,1)} %bitcast.8, f32[2,128]{1,0:T(2,128)} %bitcast.9, s32[8,64,128]{2,1,0:T(8,128)} %ids_hbm.1, s32[1,128]{1,0:T(1,128)} %bitcast.11, ...), custom_call_target="tpu_custom_call" | custom-call | tf_op jit(solution)/shard_map/solves/pallas_call | solution.py:779
  72.9 1.7 %write.1 = (f32[2,3,8,64,128]{4,3,2,1,0:T(8,128)}, f32[2,3,8,64,128]{4,3,2,1,0:T(8,128)}, f32[2,128]{1,0:T(2,128)}) custom-call(f32[2,3,8,64,128]{4,3,2,1,0:T(8,128)S(1)} %get-tuple-element.9.forward_ref, f32[2,3,8,64,128]{4,3,2,1,0:T(8,128)S(1)} %get-tuple-element.10.adjoint_ref, f32[2,128]{1,0:T(2,128)S(1)} %get-tuple-element.11.gradient_ref), custom_call_target="tpu_custom_call" | custom-call | tf_op jit(solution)/shard_map/write/pallas_call | solution.py:828

commit v4 on v3

--- a/solution.py
+++ b/solution.py
@@ -32,7 +32,7 @@
     damp, real_ref, imag_ref, cond, beside, pack_ref, mis_out, mis_in,
     basis, zb, curl, up_out, down_out, low_in, high_in,
     gram_acc, gram_out, gram_in, pack_in, grad_out, grad_in,
-    columns, hot, hot_t, field_hi, field_lo, mis_hi, mis_lo, acc,
+    columns, hot, hot_t, field_hi, field_lo, mis_hi, mis_lo, acc, hot_block, overlap,
     local_s, up_s, up_r, down_s, down_r, gram_s, gram_r, pack_s, pack_r, grad_s, grad_r,
     near_s, near_r, share_s, share_r,
 ):
@@ -210,13 +210,11 @@
             curl[c, 1, x, shifted] = f3(e1) - (zb[c, 2, x + 1, inner] - e3)
             curl[c, 2, x, shifted] = (zb[c, 1, x + 1, inner] - e2) - (zb[c, 0, x, above] - e1)
 
-    def images(t, x, keep=None):
+    def images(t, x):
         damping = damp[x]
         for c in range(2):
             b1, b2, b3 = curl[c, 0, x, shifted], curl[c, 1, x, shifted], curl[c, 2, x, shifted]
             b2p, b3p = curl[c, 1, x - 1, shifted], curl[c, 2, x - 1, shifted]
-            if keep is not None:
-                b2p, b3p = b2p * keep, b3p * keep
             parts = (
                 g3(b2) - (curl[c, 2, x, under] - b3),
                 (b3p - b3) - g3(b1),
@@ -377,8 +375,7 @@
             )
 
         def step(x, carry, inside):
-            keep = jnp.where((x == first) & (me == 0), 0.0, 1.0).astype(F32) if inside else None
-            images(t, x, keep)
+            images(t, x)
             curls(x + 1)
             precondition(t, x + 3)
             return gather(x, carry) if inside else carry
@@ -386,6 +383,9 @@
         sums = tuple(blank_sums(j) for j in wanted)
         top = min(hi - 2, last + 1)
         lax.fori_loop(lo + 1, first, lambda x, carry: step(x, carry, False), 0)
+        for c in range(2):
+            for k in range(1, 3):
+                curl[c, k, first - 1, shifted] = curl[c, k, first - 1, shifted] * valid
         sums = lax.fori_loop(first, top, lambda x, carry: step(x, carry, True), sums)
         lax.fori_loop(top, hi - 2, lambda x, carry: step(x, carry, False), 0)
         images(t, hi - 2)
@@ -563,9 +563,8 @@
         high_in[...] = jnp.zeros(high_in.shape, F32)
 
     pl.semaphore_wait(barrier, n * nf - 1)
-    for half in range(2):
-        send_down(0, half)
-        send_up(0, half)
+    send_down(0, 0)
+    send_up(0, 0)
     loads[3].wait()
     loads[4].wait()
     loads[5].wait()
@@ -577,10 +576,12 @@
         ],
         axis=0,
     )
+    pack_in[me] = pack_ref[...]
+    lax.fori_loop(0, (planes - 2) * chunks, begin_inner, 0, unroll=4)
+    send_down(0, 1)
+    send_up(0, 1)
     for copy in packs:
         copy.start()
-    pack_in[me] = pack_ref[...]
-    lax.fori_loop(0, (planes - 2) * chunks, begin_inner, 0, unroll=4)
 
     def nothing():
         pass
@@ -673,32 +674,57 @@
 
     for t in range(SWEEPS):
         sweep(t)
-    for copy in gram_start(1):
-        copy.wait()
-    combine(coefficients(1), adjoint_ref, False)
+    sums_sent = gram_start(1)
 
     high_iota = lax.broadcasted_iota(jnp.int32, (high_blocks, lanes), 0)
     low_iota = lax.broadcasted_iota(jnp.int32, (LOW, lanes), 0)
+
+    def block_rows(i, carry):
+        x, y = i // chunks, pl.multiple_of(i % chunks * 16, 16)
+        high = ids_ref[x, pl.ds(y, 16), :] >> 4
+        hot_block[i] = jnp.concatenate(
+            [jnp.where(high[r : r + 1, :] == high_iota, 1.0, 0.0) for r in range(16)], axis=0
+        ).astype(BF16)
+        return carry
+
+    def overlaps(i, carry):
+        x, y = i // chunks, pl.multiple_of(i % chunks * 16, 16)
+        at = pl.ds(y, 16)
+        field = [[forward_ref[c, comp, x, at, :] for comp in range(3)] for c in range(2)]
+        mr, mi = real_ref[x + first, at, :], imag_ref[x + first, at, :]
+        for k in range(SWEEPS):
+            qr = jnp.zeros((16, lanes), F32)
+            qi = jnp.zeros((16, lanes), F32)
+            for comp in range(3):
+                br, bi = basis[k, 0, comp, x + first, at, :], basis[k, 1, comp, x + first, at, :]
+                qr = qr + (br * field[0][comp] - bi * field[1][comp])
+                qi = qi + (br * field[1][comp] + bi * field[0][comp])
+            overlap[k, 0, x, at] = mr * qr + mi * qi
+            overlap[k, 1, x, at] = mr * qi - mi * qr
+        return carry
+
+    lax.fori_loop(0, planes * chunks, block_rows, 0, unroll=2)
+    lax.fori_loop(0, planes * chunks, overlaps, 0, unroll=2)
+    for copy in sums_sent:
+        copy.wait()
+    adjoint_steps = coefficients(1)
+
     acc[...] = jnp.zeros(acc.shape, F32)
 
     def cells(i, carry):
         x, y = i // chunks, pl.multiple_of(i % chunks * 16, 16)
+        at = pl.ds(y, 16)
         value = jnp.zeros((16, lanes), F32)
-        for comp in range(3):
-            fr, fi = forward_ref[0, comp, x, pl.ds(y, 16), :], forward_ref[1, comp, x, pl.ds(y, 16), :]
-            ar, ai = adjoint_ref[0, comp, x, pl.ds(y, 16), :], adjoint_ref[1, comp, x, pl.ds(y, 16), :]
-            value = value + (ar * fi + ai * fr)
+        for k in range(SWEEPS):
+            value = value + (adjoint_steps[k][0] * overlap[k, 1, x, at, :] + adjoint_steps[k][1] * overlap[k, 0, x, at, :])
         value = omega * value
-        ids = ids_ref[x, pl.ds(y, 16), :]
-        high, low = ids >> 4, ids & (LOW - 1)
-        hot = jnp.concatenate(
-            [jnp.where(high[r : r + 1, :] == high_iota, 1.0, 0.0) for r in range(16)], axis=0
-        ).astype(BF16)
+        low = ids_ref[x, at, :] & (LOW - 1)
         spot = jnp.concatenate(
             [jnp.where(low[r : r + 1, :] == low_iota, value[r : r + 1, :], 0.0) for r in range(16)], axis=0
         )
+        here = hot_block[i]
         acc[...] += lax.dot_general(
-            jnp.concatenate([hot, hot], axis=1), jnp.concatenate(split(spot), axis=1),
+            jnp.concatenate([here, here], axis=1), jnp.concatenate(split(spot), axis=1),
             (((1,), (1,)), ((), ())), preferred_element_type=F32,
         )
         return carry
@@ -731,6 +757,7 @@
         copy.start()
         copies.append(copy)
     grad_in[0] = own
+    combine(adjoint_steps, adjoint_ref, False)
     for copy in copies:
         copy.wait()
 
@@ -812,6 +839,8 @@
             pltpu.VMEM((slots, 2 * lanes), BF16),
             pltpu.VMEM((slots, 2 * lanes), BF16),
             pltpu.VMEM((16 * high_blocks, 16 * LOW), F32),
+            pltpu.VMEM((planes * rows // 16, 16 * high_blocks, lanes), BF16),
+            pltpu.VMEM((SWEEPS, 2, planes, rows, lanes), F32),
             dma((6,)),
             dma((SWEEPS, 2)), dma((SWEEPS, 2)), dma((SWEEPS, 2)), dma((SWEEPS, 2)),
             dma((2, n)), dma((2, n)),

time: 74.8 us -> 72.9 us (0.975)
  Pallas kernels: 73.3 us -> 71.4 us
    pallas_call x1, Pallas kernels: 71.6 us -> 69.7 us  [body(): pl.pallas_call(functools.partial(kernel, n, nf, high_blocks), out_shape=(...]
where the time goes in v4:
time: 72.9 us; the launch traced here: 72.7 us
  Pallas kernels  71.4 us (98%)
  between operations  1.29 us (2%)
    pallas_call x1, Pallas kernels, body(): pl.pallas_call(functools.partial(kernel, n, nf, high_blocks), out_shape=(...  69.7 us
    pallas_call x1, Pallas kernels, body(): pl.pallas_call(write_kernel, out_shape=(jax.ShapeDtypeStruct(field, F32),...  1.69 us

profile of v4, /device:TPU:0, one launch (start us, length us, event | category | flops | bytes accessed | tf_op | source)
XLA Modules:
  0.0 72.7 jit_solution(10608887371218353476)
XLA Ops:
  1.3 69.7 %solves.1 = (f32[2,3,8,64,128]{4,3,2,1,0:T(8,128)S(1)}, f32[2,3,8,64,128]{4,3,2,1,0:T(8,128)S(1)}, f32[2,128]{1,0:T(2,128)S(1)}) custom-call(f32[1]{0:T(128)S(6)} %copy.10.omega_ref, bf16[2,3,8,64,128]{4,3,2,1,0:T(8,128)(2,1)} %bitcast.8, f32[2,128]{1,0:T(2,128)} %bitcast.9, s32[8,64,128]{2,1,0:T(8,128)} %ids_hbm.1, s32[1,128]{1,0:T(1,128)} %bitcast.11, ...), custom_call_target="tpu_custom_call" | custom-call | tf_op jit(solution)/shard_map/solves/pallas_call | solution.py:806
  71.0 1.7 %write.1 = (f32[2,3,8,64,128]{4,3,2,1,0:T(8,128)}, f32[2,3,8,64,128]{4,3,2,1,0:T(8,128)}, f32[2,128]{1,0:T(2,128)}) custom-call(f32[2,3,8,64,128]{4,3,2,1,0:T(8,128)S(1)} %get-tuple-element.9.forward_ref, f32[2,3,8,64,128]{4,3,2,1,0:T(8,128)S(1)} %get-tuple-element.10.adjoint_ref, f32[2,128]{1,0:T(2,128)S(1)} %get-tuple-element.11.gradient_ref), custom_call_target="tpu_custom_call" | custom-call | tf_op jit(solution)/shard_map/write/pallas_call | solution.py:857

commit v5 on v4

--- a/solution.py
+++ b/solution.py
@@ -32,7 +32,7 @@
     damp, real_ref, imag_ref, cond, beside, pack_ref, mis_out, mis_in,
     basis, zb, curl, up_out, down_out, low_in, high_in,
     gram_acc, gram_out, gram_in, pack_in, grad_out, grad_in,
-    columns, hot, hot_t, field_hi, field_lo, mis_hi, mis_lo, acc, hot_block, overlap,
+    columns, hot, hot_t, field_hi, field_lo, mis_hi, mis_lo, acc, hot_block, low_block, overlap,
     local_s, up_s, up_r, down_s, down_r, gram_s, gram_r, pack_s, pack_r, grad_s, grad_r,
     near_s, near_r, share_s, share_r,
 ):
@@ -680,11 +680,14 @@
     low_iota = lax.broadcasted_iota(jnp.int32, (LOW, lanes), 0)
 
     def block_rows(i, carry):
-        x, y = i // chunks, pl.multiple_of(i % chunks * 16, 16)
-        high = ids_ref[x, pl.ds(y, 16), :] >> 4
+        x, y = i // per, pl.multiple_of(i % per * 8, 8)
+        ids = ids_ref[x, pl.ds(y, 8), :]
+        high, low = ids >> 4, ids & (LOW - 1)
         hot_block[i] = jnp.concatenate(
-            [jnp.where(high[r : r + 1, :] == high_iota, 1.0, 0.0) for r in range(16)], axis=0
+            [jnp.where(high[r : r + 1, :] == high_iota, 1.0, 0.0) for r in range(8)], axis=0
         ).astype(BF16)
+        for r in range(8):
+            low_block[i, r * LOW : (r + 1) * LOW, :] = jnp.where(low[r : r + 1, :] == low_iota, 1.0, 0.0)
         return carry
 
     def overlaps(i, carry):
@@ -703,7 +706,7 @@
             overlap[k, 1, x, at] = mr * qi - mi * qr
         return carry
 
-    lax.fori_loop(0, planes * chunks, block_rows, 0, unroll=2)
+    lax.fori_loop(0, planes * per, block_rows, 0, unroll=4)
     lax.fori_loop(0, planes * chunks, overlaps, 0, unroll=2)
     for copy in sums_sent:
         copy.wait()
@@ -712,15 +715,15 @@
     acc[...] = jnp.zeros(acc.shape, F32)
 
     def cells(i, carry):
-        x, y = i // chunks, pl.multiple_of(i % chunks * 16, 16)
-        at = pl.ds(y, 16)
-        value = jnp.zeros((16, lanes), F32)
+        x, y = i // per, pl.multiple_of(i % per * 8, 8)
+        at = pl.ds(y, 8)
+        value = jnp.zeros((8, lanes), F32)
         for k in range(SWEEPS):
-            value = value + (adjoint_steps[k][0] * overlap[k, 1, x, at, :] + adjoint_steps[k][1] * overlap[k, 0, x, at, :])
+            cr, ci = adjoint_steps[k][0][:8], adjoint_steps[k][1][:8]
+            value = value + (cr * overlap[k, 1, x, at, :] + ci * overlap[k, 0, x, at, :])
         value = omega * value
-        low = ids_ref[x, at, :] & (LOW - 1)
         spot = jnp.concatenate(
-            [jnp.where(low[r : r + 1, :] == low_iota, value[r : r + 1, :], 0.0) for r in range(16)], axis=0
+            [low_block[i, r * LOW : (r + 1) * LOW, :] * value[r : r + 1, :] for r in range(8)], axis=0
         )
         here = hot_block[i]
         acc[...] += lax.dot_general(
@@ -729,13 +732,12 @@
         )
         return carry
 
-    lax.fori_loop(0, planes * chunks, cells, 0, unroll=4)
-    wide_lane = lax.broadcasted_iota(jnp.int32, (high_blocks, 16 * LOW), 1)
-    diagonal = jnp.zeros((high_blocks, 16 * LOW), F32)
-    for r in range(16):
+    lax.fori_loop(0, planes * per, cells, 0, unroll=8)
+    wide_lane = lax.broadcasted_iota(jnp.int32, (high_blocks, 8 * LOW), 1)
+    folded = jnp.zeros((high_blocks, 8 * LOW), F32)
+    for r in range(8):
         inside = (wide_lane >= r * LOW) & (wide_lane < (r + 1) * LOW)
-        diagonal = diagonal + jnp.where(inside, acc[r * high_blocks : (r + 1) * high_blocks, :], 0.0)
-    folded = diagonal[:, :lanes] + diagonal[:, lanes:]
+        folded = folded + jnp.where(inside, acc[r * high_blocks : (r + 1) * high_blocks, :], 0.0)
     for shift in (64, 32, 16):
         folded = folded + pltpu.roll(folded, shift, 1)
     fold_lane = lax.broadcasted_iota(jnp.int32, (8, lanes), 1) // LOW
@@ -838,8 +840,9 @@
             pltpu.VMEM((cells_rows, 2 * lanes), BF16),
             pltpu.VMEM((slots, 2 * lanes), BF16),
             pltpu.VMEM((slots, 2 * lanes), BF16),
-            pltpu.VMEM((16 * high_blocks, 16 * LOW), F32),
-            pltpu.VMEM((planes * rows // 16, 16 * high_blocks, lanes), BF16),
+            pltpu.VMEM((8 * high_blocks, 8 * LOW), F32),
+            pltpu.VMEM((planes * rows // 8, 8 * high_blocks, lanes), BF16),
+            pltpu.VMEM((planes * rows // 8, 8 * LOW, lanes), F32),
             pltpu.VMEM((SWEEPS, 2, planes, rows, lanes), F32),
             dma((6,)),
             dma((SWEEPS, 2)), dma((SWEEPS, 2)), dma((SWEEPS, 2)), dma((SWEEPS, 2)),

time: 72.9 us -> 72.4 us (level)
  no operation moved by 1% of the time
where the time goes in v5:
time: 72.4 us; the launch traced here: 72.3 us
  Pallas kernels  71 us (98%)
  between operations  1.29 us (2%)
    pallas_call x1, Pallas kernels, body(): pl.pallas_call(functools.partial(kernel, n, nf, high_blocks), out_shape=(...  69.3 us
    pallas_call x1, Pallas kernels, body(): pl.pallas_call(write_kernel, out_shape=(jax.ShapeDtypeStruct(field, F32),...  1.69 us

profile of v5, /device:TPU:0, one launch (start us, length us, event | category | flops | bytes accessed | tf_op | source)
XLA Modules:
  0.0 72.3 jit_solution(9132113828770851974)
XLA Ops:
  1.3 69.3 %solves.1 = (f32[2,3,8,64,128]{4,3,2,1,0:T(8,128)S(1)}, f32[2,3,8,64,128]{4,3,2,1,0:T(8,128)S(1)}, f32[2,128]{1,0:T(2,128)S(1)}) custom-call(f32[1]{0:T(128)S(6)} %copy.10.omega_ref, bf16[2,3,8,64,128]{4,3,2,1,0:T(8,128)(2,1)} %bitcast.8, f32[2,128]{1,0:T(2,128)} %bitcast.9, s32[8,64,128]{2,1,0:T(8,128)} %ids_hbm.1, s32[1,128]{1,0:T(1,128)} %bitcast.11, ...), custom_call_target="tpu_custom_call" | custom-call | tf_op jit(solution)/shard_map/solves/pallas_call | solution.py:808
  70.6 1.7 %write.1 = (f32[2,3,8,64,128]{4,3,2,1,0:T(8,128)}, f32[2,3,8,64,128]{4,3,2,1,0:T(8,128)}, f32[2,128]{1,0:T(2,128)}) custom-call(f32[2,3,8,64,128]{4,3,2,1,0:T(8,128)S(1)} %get-tuple-element.9.forward_ref, f32[2,3,8,64,128]{4,3,2,1,0:T(8,128)S(1)} %get-tuple-element.10.adjoint_ref, f32[2,128]{1,0:T(2,128)S(1)} %get-tuple-element.11.gradient_ref), custom_call_target="tpu_custom_call" | custom-call | tf_op jit(solution)/shard_map/write/pallas_call | solution.py:860

commit v6 on v5

--- a/solution.py
+++ b/solution.py
@@ -284,19 +284,6 @@
         lo, hi = rows_of(t, half)
         at = slice(lo, hi)
 
-        @pl.when(me > 0)
-        def _():
-            up_copy(t, half).wait_recv()
-
-        for c in range(2):
-            b2p = (low_in[t, place_of(t, half, c, 0)] - zb[c, 2, first, at]) * valid
-            b3p = (zb[c, 1, first, at] - low_in[t, place_of(t, half, c, 1)]) * valid
-            basis[t + 1, c, 1, first, at] += b3p
-            basis[t + 1, c, 2, first, at] -= b2p
-        if t < SWEEPS - 1:
-            precondition(t + 1, first, at)
-            send_down(t + 1, half)
-
         @pl.when(me < n - 1)
         def _():
             down_copy(t, half).wait_recv()
@@ -311,6 +298,19 @@
         if t < SWEEPS - 1:
             precondition(t + 1, last, at)
             send_up(t + 1, half)
+
+        @pl.when(me > 0)
+        def _():
+            up_copy(t, half).wait_recv()
+
+        for c in range(2):
+            b2p = (low_in[t, place_of(t, half, c, 0)] - zb[c, 2, first, at]) * valid
+            b3p = (zb[c, 1, first, at] - low_in[t, place_of(t, half, c, 1)]) * valid
+            basis[t + 1, c, 1, first, at] += b3p
+            basis[t + 1, c, 2, first, at] -= b2p
+        if t < SWEEPS - 1:
+            precondition(t + 1, first, at)
+            send_down(t + 1, half)
 
     def forward_sweep(t, before, between):
         sweep_inner(t)

time: 72.4 us -> 69 us (0.953)
  Pallas kernels: 71 us -> 67.6 us
    pallas_call x1, Pallas kernels: 69.3 us -> 65.9 us  [body(): pl.pallas_call(functools.partial(kernel, n, nf, high_blocks), out_shape=(...]
where the time goes in v6:
time: 69 us; the launch traced here: 68.9 us
  Pallas kernels  67.6 us (98%)
  between operations  1.29 us (2%)
    pallas_call x1, Pallas kernels, body(): pl.pallas_call(functools.partial(kernel, n, nf, high_blocks), out_shape=(...  65.9 us
    pallas_call x1, Pallas kernels, body(): pl.pallas_call(write_kernel, out_shape=(jax.ShapeDtypeStruct(field, F32),...  1.69 us

profile of v6, /device:TPU:0, one launch (start us, length us, event | category | flops | bytes accessed | tf_op | source)
XLA Modules:
  0.0 68.9 jit_solution(2685908085435145060)
XLA Ops:
  1.3 65.9 %solves.1 = (f32[2,3,8,64,128]{4,3,2,1,0:T(8,128)S(1)}, f32[2,3,8,64,128]{4,3,2,1,0:T(8,128)S(1)}, f32[2,128]{1,0:T(2,128)S(1)}) custom-call(f32[1]{0:T(128)S(6)} %copy.10.omega_ref, bf16[2,3,8,64,128]{4,3,2,1,0:T(8,128)(2,1)} %bitcast.8, f32[2,128]{1,0:T(2,128)} %bitcast.9, s32[8,64,128]{2,1,0:T(8,128)} %ids_hbm.1, s32[1,128]{1,0:T(1,128)} %bitcast.11, ...), custom_call_target="tpu_custom_call" | custom-call | tf_op jit(solution)/shard_map/solves/pallas_call | solution.py:808
  67.2 1.7 %write.1 = (f32[2,3,8,64,128]{4,3,2,1,0:T(8,128)}, f32[2,3,8,64,128]{4,3,2,1,0:T(8,128)}, f32[2,128]{1,0:T(2,128)}) custom-call(f32[2,3,8,64,128]{4,3,2,1,0:T(8,128)S(1)} %get-tuple-element.9.forward_ref, f32[2,3,8,64,128]{4,3,2,1,0:T(8,128)S(1)} %get-tuple-element.10.adjoint_ref, f32[2,128]{1,0:T(2,128)S(1)} %get-tuple-element.11.gradient_ref), custom_call_target="tpu_custom_call" | custom-call | tf_op jit(solution)/shard_map/write/pallas_call | solution.py:860

commit v7 on v6

--- a/solution.py
+++ b/solution.py
@@ -577,9 +577,11 @@
         axis=0,
     )
     pack_in[me] = pack_ref[...]
-    lax.fori_loop(0, (planes - 2) * chunks, begin_inner, 0, unroll=4)
+    half_way = (planes - 2) // 2 * chunks
+    lax.fori_loop(0, half_way, begin_inner, 0, unroll=4)
     send_down(0, 1)
     send_up(0, 1)
+    lax.fori_loop(half_way, (planes - 2) * chunks, begin_inner, 0, unroll=4)
     for copy in packs:
         copy.start()
 

time: 69 us -> 69 us (level)
  no operation moved by 1% of the time
where the time goes in v7:
time: 69 us; the launch traced here: 68.9 us
  Pallas kernels  67.6 us (98%)
  between operations  1.29 us (2%)
    pallas_call x1, Pallas kernels, body(): pl.pallas_call(functools.partial(kernel, n, nf, high_blocks), out_shape=(...  65.9 us
    pallas_call x1, Pallas kernels, body(): pl.pallas_call(write_kernel, out_shape=(jax.ShapeDtypeStruct(field, F32),...  1.69 us

profile of v7, /device:TPU:0, one launch (start us, length us, event | category | flops | bytes accessed | tf_op | source)
XLA Modules:
  0.0 68.9 jit_solution(9014410054487977993)
XLA Ops:
  1.3 65.9 %solves.1 = (f32[2,3,8,64,128]{4,3,2,1,0:T(8,128)S(1)}, f32[2,3,8,64,128]{4,3,2,1,0:T(8,128)S(1)}, f32[2,128]{1,0:T(2,128)S(1)}) custom-call(f32[1]{0:T(128)S(6)} %copy.10.omega_ref, bf16[2,3,8,64,128]{4,3,2,1,0:T(8,128)(2,1)} %bitcast.8, f32[2,128]{1,0:T(2,128)} %bitcast.9, s32[8,64,128]{2,1,0:T(8,128)} %ids_hbm.1, s32[1,128]{1,0:T(1,128)} %bitcast.11, ...), custom_call_target="tpu_custom_call" | custom-call | tf_op jit(solution)/shard_map/solves/pallas_call | solution.py:810
  67.2 1.7 %write.1 = (f32[2,3,8,64,128]{4,3,2,1,0:T(8,128)}, f32[2,3,8,64,128]{4,3,2,1,0:T(8,128)}, f32[2,128]{1,0:T(2,128)}) custom-call(f32[2,3,8,64,128]{4,3,2,1,0:T(8,128)S(1)} %get-tuple-element.9.forward_ref, f32[2,3,8,64,128]{4,3,2,1,0:T(8,128)S(1)} %get-tuple-element.10.adjoint_ref, f32[2,128]{1,0:T(2,128)S(1)} %get-tuple-element.11.gradient_ref), custom_call_target="tpu_custom_call" | custom-call | tf_op jit(solution)/shard_map/write/pallas_call | solution.py:862
